TPU v7x, 32 devices: a whole 2x2x4 slice. The times are simulated.
32 devices in a mesh: fsdp: 8 (over z, core), ctx: 4 (over y, x).
Axes of the slice: x: 2, y: 2, z: 4, core: 2. Of those that a mesh axis runs over, the one named last changes fastest.
Arguments:
- tokens: bfloat16 [8, 4096, 1088], P('fsdp', 'ctx'), may hold values from -6 to 6
- cotangent: bfloat16 [8, 4096, 1088], P('fsdp', 'ctx'), may hold values from -6 to 6
- lengths: int32 [8], P('fsdp'), may hold values from 1024 to 4096, as said below
- block_order: int32 [8, 8], P('fsdp'), may hold values from 0 to 7, each once within a row
- ln1_gain: float32 [2, 1088], P(None, 'fsdp'), may hold values from 0.25 to 1.75
- ln1_bias: float32 [2, 1088], P(None, 'fsdp'), may hold values from -1 to 1
- qkv_weight: float32 [2, 1088, 3264], P(None, 'fsdp'), may hold values from -0.1875 to 0.1875
- q_bias: float32 [2, 1088], P(None, 'fsdp'), may hold values from -1.5 to 1.5
- v_bias: float32 [2, 1088], P(None, 'fsdp'), may hold values from -1.5 to 1.5
- out_weight: float32 [2, 1088, 1088], P(None, 'fsdp'), may hold values from -1.5 to 1.5
- out_bias: float32 [2, 1088], P(None, 'fsdp'), may hold values from -1 to 1
- ln2_gain: float32 [2, 1088], P(None, 'fsdp'), may hold values from 0.25 to 1.75
- ln2_bias: float32 [2, 1088], P(None, 'fsdp'), may hold values from -1 to 1
- up_weight: float32 [2, 1088, 4352], P(None, 'fsdp'), may hold values from -0.1875 to 0.1875
- up_bias: float32 [2, 4352], P(None, 'fsdp'), may hold values from -1.5 to 1.5
- down_weight: float32 [2, 4352, 1088], P(None, 'fsdp'), may hold values from -0.09375 to 0.09375
- down_bias: float32 [2, 1088], P(None, 'fsdp'), may hold values from -1 to 1
Outputs:
- activations: bfloat16 [8, 4096, 1088], P('fsdp', 'ctx')
- tokens_grad: float32 [8, 4096, 1088], P('fsdp', 'ctx')
- ln1_gain_grad: float32 [2, 1088], P(None, 'fsdp')
- ln1_bias_grad: float32 [2, 1088], P(None, 'fsdp')
- qkv_weight_grad: float32 [2, 1088, 3264], P(None, 'fsdp')
- q_bias_grad: float32 [2, 1088], P(None, 'fsdp')
- v_bias_grad: float32 [2, 1088], P(None, 'fsdp')
- out_weight_grad: float32 [2, 1088, 1088], P(None, 'fsdp')
- out_bias_grad: float32 [2, 1088], P(None, 'fsdp')
- ln2_gain_grad: float32 [2, 1088], P(None, 'fsdp')
- ln2_bias_grad: float32 [2, 1088], P(None, 'fsdp')
- up_weight_grad: float32 [2, 1088, 4352], P(None, 'fsdp')
- up_bias_grad: float32 [2, 4352], P(None, 'fsdp')
- down_weight_grad: float32 [2, 4352, 1088], P(None, 'fsdp')
- down_bias_grad: float32 [2, 1088], P(None, 'fsdp')
Inputs may be any that keep to these rules, and one draw needn't show every extreme that they name: Some slot holds exactly 4096 valid tokens and some exactly 1024; valid tokens are the first lengths of the sequence positions. `block_order`: each row names every block of its slot once.
All inputs are finite; a program needn't handle non-finite values.
Results may differ from a plain program's by a relative error of at most 0.019.
Values may be sent and summed in bfloat16 or wider, within the bound.
A program may use at most 512 MiB of HBM per device.

v0:
```python
import jax
import jax.numpy as jnp
from jax import lax
from jax.sharding import PartitionSpec as P

HEADS = 17


MASKED = -1000000000.0
EPSILON = 1e-05


def layer_norm(values, norm_gain, norm_bias):
    average = jnp.mean(values, axis=-1, keepdims=True)
    centred = values - average
    variance = jnp.mean(centred * centred, axis=-1, keepdims=True)
    return centred * lax.rsqrt(variance + EPSILON) * norm_gain + norm_bias


def exact_gelu(value_in):
    return jax.nn.gelu(value_in, approximate=False)


def fetch_forward(masters, layer):
    parts = [weight[layer].astype(jnp.bfloat16) for weight in masters]
    return (
        lax.all_gather(parts[0], "fsdp", axis=0, tiled=True),
        lax.all_gather(parts[1], "fsdp", axis=0, tiled=True),
        lax.all_gather(parts[2], "fsdp", axis=0, tiled=True),
        lax.all_gather(parts[3], "fsdp", axis=0, tiled=True),
        lax.all_gather(parts[4], "fsdp", axis=0, tiled=True),
        lax.all_gather(parts[5], "fsdp", axis=0, tiled=True),
        lax.all_gather(parts[6], "fsdp", axis=0, tiled=True),
        lax.all_gather(parts[7], "fsdp", axis=0, tiled=True),
        lax.all_gather(parts[8], "fsdp", axis=0, tiled=True),
        lax.all_gather(parts[9], "fsdp", axis=0, tiled=True),
        lax.all_gather(parts[10], "fsdp", axis=0, tiled=True),
        lax.all_gather(parts[11], "fsdp", axis=0, tiled=True),
        lax.all_gather(parts[12], "fsdp", axis=0, tiled=True),
    )


def fetch_backward(masters, layer):
    parts = [weight[layer].astype(jnp.bfloat16) for weight in masters]
    return (
        lax.all_gather(parts[0], "fsdp", axis=0, tiled=True),
        lax.all_gather(parts[1], "fsdp", axis=0, tiled=True),
        lax.all_gather(parts[2], "fsdp", axis=0, tiled=True),
        lax.all_gather(parts[3], "fsdp", axis=0, tiled=True),
        lax.all_gather(parts[4], "fsdp", axis=0, tiled=True),
        lax.all_gather(parts[5], "fsdp", axis=0, tiled=True),
        lax.all_gather(parts[6], "fsdp", axis=0, tiled=True),
        lax.all_gather(parts[7], "fsdp", axis=0, tiled=True),
        lax.all_gather(parts[8], "fsdp", axis=0, tiled=True),
        lax.all_gather(parts[9], "fsdp", axis=0, tiled=True),
        lax.all_gather(parts[10], "fsdp", axis=0, tiled=True),
        lax.all_gather(parts[11], "fsdp", axis=0, tiled=True),
        lax.all_gather(parts[12], "fsdp", axis=0, tiled=True),
    )


def reduce_grads(grads):
    owned = (
        lax.psum_scatter(
            grads[0].astype(jnp.bfloat16), "fsdp", scatter_dimension=0, tiled=True
        ).astype(jnp.float32),
        lax.psum_scatter(
            grads[1].astype(jnp.bfloat16), "fsdp", scatter_dimension=0, tiled=True
        ).astype(jnp.float32),
        lax.psum_scatter(
            grads[2].astype(jnp.bfloat16), "fsdp", scatter_dimension=0, tiled=True
        ).astype(jnp.float32),
        lax.psum_scatter(
            grads[3].astype(jnp.bfloat16), "fsdp", scatter_dimension=0, tiled=True
        ).astype(jnp.float32),
        lax.psum_scatter(
            grads[4].astype(jnp.bfloat16), "fsdp", scatter_dimension=0, tiled=True
        ).astype(jnp.float32),
        lax.psum_scatter(
            grads[5].astype(jnp.bfloat16), "fsdp", scatter_dimension=0, tiled=True
        ).astype(jnp.float32),
        lax.psum_scatter(
            grads[6].astype(jnp.bfloat16), "fsdp", scatter_dimension=0, tiled=True
        ).astype(jnp.float32),
        lax.psum_scatter(
            grads[7].astype(jnp.bfloat16), "fsdp", scatter_dimension=0, tiled=True
        ).astype(jnp.float32),
        lax.psum_scatter(
            grads[8].astype(jnp.bfloat16), "fsdp", scatter_dimension=0, tiled=True
        ).astype(jnp.float32),
        lax.psum_scatter(
            grads[9].astype(jnp.bfloat16), "fsdp", scatter_dimension=0, tiled=True
        ).astype(jnp.float32),
        lax.psum_scatter(
            grads[10].astype(jnp.bfloat16), "fsdp", scatter_dimension=0, tiled=True
        ).astype(jnp.float32),
        lax.psum_scatter(
            grads[11].astype(jnp.bfloat16), "fsdp", scatter_dimension=0, tiled=True
        ).astype(jnp.float32),
        lax.psum_scatter(
            grads[12].astype(jnp.bfloat16), "fsdp", scatter_dimension=0, tiled=True
        ).astype(jnp.float32),
    )
    column_share = (
        lax.psum_scatter(
            owned[2].astype(jnp.bfloat16), "ctx", scatter_dimension=1, tiled=True
        ).astype(jnp.float32),
        lax.psum_scatter(
            owned[5].astype(jnp.bfloat16), "ctx", scatter_dimension=1, tiled=True
        ).astype(jnp.float32),
        lax.psum_scatter(
            owned[9].astype(jnp.bfloat16), "ctx", scatter_dimension=1, tiled=True
        ).astype(jnp.float32),
        lax.psum_scatter(
            owned[11].astype(jnp.bfloat16), "ctx", scatter_dimension=1, tiled=True
        ).astype(jnp.float32),
    )
    vectors = lax.psum(
        (
            owned[0],
            owned[1],
            owned[3],
            owned[4],
            owned[6],
            owned[7],
            owned[8],
            owned[10],
            owned[12],
        ),
        "ctx",
    )
    matrices = (
        lax.all_gather(column_share[0].astype(jnp.bfloat16), "ctx", axis=1, tiled=True).astype(
            jnp.float32
        ),
        lax.all_gather(column_share[1].astype(jnp.bfloat16), "ctx", axis=1, tiled=True).astype(
            jnp.float32
        ),
        lax.all_gather(column_share[2].astype(jnp.bfloat16), "ctx", axis=1, tiled=True).astype(
            jnp.float32
        ),
        lax.all_gather(column_share[3].astype(jnp.bfloat16), "ctx", axis=1, tiled=True).astype(
            jnp.float32
        ),
    )
    return (
        vectors[0],
        vectors[1],
        matrices[0],
        vectors[2],
        vectors[3],
        matrices[1],
        vectors[4],
        vectors[5],
        vectors[6],
        matrices[2],
        vectors[7],
        matrices[3],
        vectors[8],
    )


def local(
    tokens,
    cotangent,
    lengths,
    block_order,
    ln1_gain,
    ln1_bias,
    qkv_weight,
    q_bias,
    v_bias,
    out_weight,
    out_bias,
    ln2_gain,
    ln2_bias,
    up_weight,
    up_bias,
    down_weight,
    down_bias,
):
    masters = (
        ln1_gain,
        ln1_bias,
        qkv_weight,
        q_bias,
        v_bias,
        out_weight,
        out_bias,
        ln2_gain,
        ln2_bias,
        up_weight,
        up_bias,
        down_weight,
        down_bias,
    )
    slots, local_len, width = tokens.shape
    ctx_count = lax.axis_size("ctx")
    ctx_place = lax.axis_index("ctx")
    block_len = local_len // 2
    full_len = local_len * ctx_count
    every_pos = (
        block_order[:, :, None] * block_len + jnp.arange(block_len, dtype=jnp.int32)[None, None, :]
    ).reshape(slots, full_len)
    own_pos = lax.dynamic_slice_in_dim(every_pos, ctx_place * local_len, local_len, 1)
    live = (own_pos < lengths[:, None]).astype(jnp.float32)
    length_col = lengths[:, None, None, None]
    groups = HEADS
    depth = width // groups
    factor = depth ** (-0.5)
    total_rows = slots * local_len
    layers = ln1_gain.shape[0]
    f32 = jnp.float32
    bf16 = jnp.bfloat16

    def allowed_of(key_places):
        return (key_places[:, None, None, :] <= own_pos[:, None, :, None]) & (
            key_places[:, None, None, :] < length_col
        )

    stream = tokens.astype(f32).reshape(total_rows, width)
    records = []
    for layer in range(layers):
        fetched = fetch_forward(masters, layer)
        (
            gain_one,
            bias_one,
            qkv_w,
            q_b,
            v_b,
            out_w,
            out_b,
            gain_two,
            bias_two,
            up_w,
            up_b,
            down_w,
            down_b,
        ) = fetched
        normed = layer_norm(stream, gain_one.astype(f32), bias_one.astype(f32)).astype(bf16)
        qkv_bias = jnp.concatenate([q_b, jnp.zeros_like(q_b), v_b]).astype(f32)
        projected = (jnp.dot(normed, qkv_w, preferred_element_type=f32) + qkv_bias).astype(bf16)
        queries = projected[:, :width].reshape(slots, local_len, groups, depth)
        key_local = projected[:, width:].reshape(slots, local_len, 2 * width)

        def forward_block(state, key_part, key_places, queries=queries):
            allowed = allowed_of(key_places)
            count = key_part.shape[1]
            accum, running, totals = state
            key_heads = key_part[..., :width].reshape(slots, count, groups, depth)
            value_heads = key_part[..., width:].reshape(slots, count, groups, depth)
            scores = (
                jnp.einsum("sqhe,skhe->shqk", queries, key_heads, preferred_element_type=f32)
                * factor
            )
            scores = jnp.where(allowed, scores, MASKED)
            newest = jnp.maximum(running, jnp.max(scores, axis=-1))
            carried = jnp.exp(running - newest)
            soft_part = jnp.where(allowed, jnp.exp(scores - newest[..., None]), 0.0)
            totals = totals * carried + jnp.sum(soft_part, axis=-1)
            update = jnp.einsum(
                "shqk,skhe->shqe", soft_part.astype(bf16), value_heads, preferred_element_type=f32
            )
            return (accum * carried[..., None] + update, newest, totals)

        def fold_keys(state, piece, start, forward_block=forward_block):
            count = piece.shape[1]
            height = 512

            def visit(index, inner):
                key_part = lax.dynamic_slice_in_dim(piece, index * height, height, 1)
                key_places = lax.dynamic_slice_in_dim(every_pos, index * height, height, 1)
                return forward_block(inner, key_part, key_places)

            return lax.fori_loop(0, count // height, visit, state)

        initial = (
            jnp.zeros((slots, groups, local_len, depth), f32),
            jnp.full((slots, groups, local_len), -1e30, f32),
            jnp.zeros((slots, groups, local_len), f32),
        )
        accum, running, totals = fold_keys(
            initial, lax.all_gather(key_local, "ctx", axis=1, tiled=True), jnp.int32(0)
        )
        mixed_heads = accum / totals[..., None]
        log_total = running + jnp.log(totals)
        mixed = jnp.transpose(mixed_heads, (0, 2, 1, 3)).reshape(total_rows, width)
        mixed_low = mixed.astype(bf16)
        middle = stream + jnp.dot(mixed_low, out_w, preferred_element_type=f32) + out_b.astype(f32)
        normed_two = layer_norm(middle, gain_two.astype(f32), bias_two.astype(f32)).astype(bf16)
        hidden_pre = jnp.dot(normed_two, up_w, preferred_element_type=f32) + up_b.astype(f32)
        hidden = exact_gelu(hidden_pre).astype(bf16)
        records.append(
            (
                stream,
                normed,
                queries,
                key_local,
                mixed,
                mixed_low,
                log_total,
                middle,
                normed_two,
                hidden_pre,
                hidden,
                fetched,
            )
        )
        stream = middle + jnp.dot(hidden, down_w, preferred_element_type=f32) + down_b.astype(f32)
    activations = (stream.reshape(slots, local_len, width) * live[..., None]).astype(bf16)
    grad = (cotangent.astype(f32) * live[..., None]).reshape(total_rows, width)
    collected = [None] * layers
    for layer in reversed(range(layers)):
        (
            stream_in,
            normed,
            queries,
            key_local,
            mixed,
            mixed_low,
            log_total,
            middle,
            normed_two,
            hidden_pre,
            hidden,
            fetched,
        ) = records[layer]
        weights = fetch_backward(masters, layer)
        (
            gain_one,
            bias_one,
            qkv_w,
            q_b,
            v_b,
            out_w,
            out_b,
            gain_two,
            bias_two,
            up_w,
            up_b,
            down_w,
            down_b,
        ) = weights
        grad_low = grad.astype(bf16)
        d_down_bias = jnp.sum(grad_low.astype(f32), axis=0)
        d_down = jnp.einsum("rf,rd->fd", hidden, grad_low, preferred_element_type=f32)
        d_hidden = jnp.einsum("rd,fd->rf", grad_low, down_w, preferred_element_type=f32)
        gelu_pull = jax.vjp(exact_gelu, hidden_pre)[1]
        d_pre = gelu_pull(d_hidden)[0].astype(bf16)
        d_up_bias = jnp.sum(d_pre.astype(f32), axis=0)
        d_up = jnp.einsum("rd,rf->df", normed_two, d_pre, preferred_element_type=f32)
        d_normed_two = jnp.einsum("rf,df->rd", d_pre, up_w, preferred_element_type=f32)
        norm_pull_two = jax.vjp(layer_norm, middle, gain_two.astype(f32), bias_two.astype(f32))[1]
        d_middle, d_gain_two, d_bias_two = norm_pull_two(d_normed_two)
        grad_mid = grad + d_middle
        mid_low = grad_mid.astype(bf16)
        d_out_bias = jnp.sum(mid_low.astype(f32), axis=0)
        d_out = jnp.einsum("rd,re->de", mixed_low, mid_low, preferred_element_type=f32)
        d_mixed = jnp.einsum("re,de->rd", mid_low, out_w, preferred_element_type=f32).astype(bf16)
        grad_heads = d_mixed.reshape(slots, local_len, groups, depth)
        delta = jnp.transpose(
            jnp.sum(
                grad_heads.astype(f32) * mixed.reshape(slots, local_len, groups, depth), axis=-1
            ),
            (0, 2, 1),
        )
        key_full = lax.all_gather(key_local, "ctx", axis=1, tiled=True)
        height = 512

        def back_visit(
            index,
            inner,
            queries=queries,
            grad_heads=grad_heads,
            delta=delta,
            log_total=log_total,
            key_full=key_full,
            height=height,
        ):
            dq_acc, dkv_acc = inner
            key_part = lax.dynamic_slice_in_dim(key_full, index * height, height, 1)
            key_places = lax.dynamic_slice_in_dim(every_pos, index * height, height, 1)
            allowed = allowed_of(key_places)
            key_heads = key_part[..., :width].reshape(slots, height, groups, depth)
            value_heads = key_part[..., width:].reshape(slots, height, groups, depth)
            scores = (
                jnp.einsum("sqhe,skhe->shqk", queries, key_heads, preferred_element_type=f32)
                * factor
            )
            scores = jnp.where(allowed, scores, MASKED)
            soft_part = jnp.where(allowed, jnp.exp(scores - log_total[..., None]), 0.0)
            soft_low = soft_part.astype(bf16)
            d_soft = jnp.einsum(
                "sqhe,skhe->shqk", grad_heads, value_heads, preferred_element_type=f32
            )
            d_scores = (soft_part * (d_soft - delta[..., None])).astype(bf16)
            dq_part = (
                jnp.einsum("shqk,skhe->shqe", d_scores, key_heads, preferred_element_type=f32)
                * factor
            )
            dk_part = (
                jnp.einsum("shqk,sqhe->skhe", d_scores, queries, preferred_element_type=f32)
                * factor
            )
            dv_part = jnp.einsum(
                "shqk,sqhe->skhe", soft_low, grad_heads, preferred_element_type=f32
            )
            dkv_part = jnp.concatenate(
                [dk_part.reshape(slots, height, width), dv_part.reshape(slots, height, width)],
                axis=-1,
            )
            dq_part, dkv_part = (dq_part, dkv_part)
            return (
                dq_acc + dq_part,
                lax.dynamic_update_slice_in_dim(dkv_acc, dkv_part, index * height, 1),
            )

        start_state = (
            jnp.zeros((slots, groups, local_len, depth), f32),
            jnp.zeros((slots, full_len, 2 * width), f32),
        )
        dq_acc, dkv_acc = lax.fori_loop(0, full_len // height, back_visit, start_state)
        key_grads = lax.psum_scatter(
            dkv_acc.astype(jnp.bfloat16), "ctx", scatter_dimension=1, tiled=True
        ).astype(jnp.float32)
        d_query = jnp.transpose(dq_acc, (0, 2, 1, 3)).reshape(total_rows, width)
        d_proj = jnp.concatenate(
            [d_query, key_grads.reshape(total_rows, 2 * width)], axis=-1
        ).astype(bf16)
        d_proj_wide = d_proj.astype(f32)
        d_q_bias = jnp.sum(d_proj_wide[:, :width], axis=0)
        d_v_bias = jnp.sum(d_proj_wide[:, 2 * width :], axis=0)
        d_qkv = jnp.einsum("rd,rc->dc", normed, d_proj, preferred_element_type=f32)
        d_normed = jnp.einsum("rc,dc->rd", d_proj, qkv_w, preferred_element_type=f32)
        norm_pull_one = jax.vjp(layer_norm, stream_in, gain_one.astype(f32), bias_one.astype(f32))[
            1
        ]
        d_stream, d_gain_one, d_bias_one = norm_pull_one(d_normed)
        grad = grad_mid + d_stream
        grads = (
            d_gain_one,
            d_bias_one,
            d_qkv,
            d_q_bias,
            d_v_bias,
            d_out,
            d_out_bias,
            d_gain_two,
            d_bias_two,
            d_up,
            d_up_bias,
            d_down,
            d_down_bias,
        )
        collected[layer] = reduce_grads(grads)
    tokens_grad = grad.reshape(slots, local_len, width)
    stacked = [
        jnp.stack([collected[layer][member] for layer in range(layers)]) for member in range(13)
    ]
    return (
        activations,
        tokens_grad,
        stacked[0],
        stacked[1],
        stacked[2],
        stacked[3],
        stacked[4],
        stacked[5],
        stacked[6],
        stacked[7],
        stacked[8],
        stacked[9],
        stacked[10],
        stacked[11],
        stacked[12],
    )


def solution(mesh):
    placed = (
        P("fsdp", "ctx", None),
        P("fsdp", "ctx", None),
        P("fsdp"),
        P("fsdp", None),
        P(None, "fsdp"),
        P(None, "fsdp"),
        P(None, "fsdp", None),
        P(None, "fsdp"),
        P(None, "fsdp"),
        P(None, "fsdp", None),
        P(None, "fsdp"),
        P(None, "fsdp"),
        P(None, "fsdp"),
        P(None, "fsdp", None),
        P(None, "fsdp"),
        P(None, "fsdp", None),
        P(None, "fsdp"),
    )
    return jax.shard_map(
        local,
        mesh=mesh,
        in_specs=placed,
        out_specs=(
            P("fsdp", "ctx", None),
            P("fsdp", "ctx", None),
            P(None, "fsdp"),
            P(None, "fsdp"),
            P(None, "fsdp", None),
            P(None, "fsdp"),
            P(None, "fsdp"),
            P(None, "fsdp", None),
            P(None, "fsdp"),
            P(None, "fsdp"),
            P(None, "fsdp"),
            P(None, "fsdp", None),
            P(None, "fsdp"),
            P(None, "fsdp", None),
            P(None, "fsdp"),
        ),
        check_vma=False,
    )
```

profile of v0, /device:TPU:0, one launch (start us, length us, event | category | flops | bytes accessed | tf_op | source)
XLA Modules:
  0.0 4012.6 jit_solution(6075065393010851106)
XLA Ops:
  18.0 34.3 all-reduce.42
  54.1 34.0 all-gather.53.cloned.1.call-done
  125.4 146.5 %all-gather.55.cloned.1.call-done = bf16[4096,2176]{0,1:T(8,128)(2,1)} async-done(((bf16[1024,2176]{0,1:T(8,128)(2,1)}), bf16[4096,2176]{0,1:T(8,128)(2,1)}) %all-gather.55.cloned.1.call-update) | async-done | bytes 17825808 | tf_op jit(solution)/shard_map/all_gather | solution.py:283
  271.9 428.1 %while.68 = (s32[]{:T(128)}, f32[1,17,1024,64]{2,3,1,0:T(8,128)}, f32[1,17,1024]{2,1,0:T(8,128)S(1)}, f32[1,17,1024]{2,1,0:T(8,128)S(1)}, s32[1,4096]{1,0:T(1,12...) while((s32[]{:T(128)}, f32[1,17,1024,64]{2,3,1,0:T(8,128)}, ...), condition=%wide.region_5.6_spmd.clone, body=%wide.region_2.5_spmd.clone.sunk | while | flops 2402064896 | bytes 128005336 | solution.py:275
  714.7 57.1 %multiply_convert_fusion.1 = (bf16[1024,4352]{1,0:T(8,128)(2,1)}, f32[1024,4352]{1,0:T(8,128)}, f32[1024,4352]{1,0:T(8,128)}) fusion(f32[4352]{0:T(1024)S(1)} %copy-done.93, bf16[1,1088,4352]{2,1,0:T(8,128)(2,1)} %all-gather.59.cloned.1.call-done, bf16[1024,1088]{0,1:T(8,128)(2,1)S(1)} %add_convert_fusion.8.clone.2), kind=kOutput, calls=%fused_computation.123 | convolution fusion | flops 9991356416 | bytes 56280064 | tf_op jit(solution)/shard_map/dot_general | solution.py:291
  816.7 162.8 %all-gather.65.cloned.1.call-done = bf16[4096,2176]{0,1:T(8,128)(2,1)} async-done(((bf16[1024,2176]{0,1:T(8,128)(2,1)}), bf16[4096,2176]{0,1:T(8,128)(2,1)}) %all-gather.65.cloned.1.call-update) | async-done | bytes 17825808 | tf_op jit(solution)/shard_map/all_gather | solution.py:283
  979.5 432.4 %while.69 = (s32[]{:T(128)}, f32[1,17,1024,64]{2,3,1,0:T(8,128)}, f32[1,17,1024]{2,1,0:T(8,128)S(1)}, f32[1,17,1024]{2,1,0:T(8,128)S(1)}, s32[1,4096]{1,0:T(1,12...) while((s32[]{:T(128)}, f32[1,17,1024,64]{2,3,1,0:T(8,128)}, ...), condition=%wide.region_13.14_spmd.clone, body=%wide.region_10.13_spmd.clone.sunk | while | flops 2402064896 | bytes 128005336 | solution.py:275
  1429.0 58.1 %multiply_convert_fusion = (bf16[1024,4352]{1,0:T(8,128)(2,1)}, f32[1024,4352]{1,0:T(8,128)}, f32[1024,4352]{1,0:T(8,128)}) fusion(f32[4352]{0:T(1024)S(1)} %copy-done.95, bf16[1,1088,4352]{2,1,0:T(8,128)(2,1)} %all-gather.69.cloned.1.call-done, bf16[1024,1088]{0,1:T(8,128)(2,1)} %add_convert_fusion.12.clone.4), kind=kOutput, calls=%fused_computation.110 | convolution fusion | flops 9991356416 | bytes 56280064 | tf_op jit(solution)/shard_map/dot_general | solution.py:291
  1487.1 23.5 fusion.185
  1545.1 664.5 %while.70 = (s32[]{:T(128)}, f32[1,17,1024,64]{2,3,1,0:T(8,128)}, bf16[1,4096,2176]{1,2,0:T(8,128)(2,1)}, s32[1,4096]{1,0:T(1,128)}, s32[1,1024]{1,0:T(1,128)S(1...) while((s32[]{:T(128)}, f32[1,17,1024,64]{2,3,1,0:T(8,128)}, ...), condition=%wide.region_20.21_spmd.clone, body=%wide.region_19.20_spmd.clone.sunk | while | flops 5821170176 | bytes 205546800 | solution.py:422
  2249.7 122.4 %reduce-scatter.35.cloned.1.call-done = bf16[1,1024,2176]{1,2,0:T(8,128)(2,1)} async-done(((bf16[1,4096,2176]{1,2,0:T(8,128)(2,1)}), bf16[1,1024,2176]{1,2,0:T(8,128)(2,1)}) %reduce-scatter.35.cloned.1.call-update) | async-done | bytes 4456464 | tf_op jit(solution)/shard_map/reduce_scatter | solution.py:423
  2414.0 28.5 fusion.186
  2527.1 53.3 %reduce-scatter.49.cloned.1.call-done = bf16[544,1088]{1,0:T(8,128)(2,1)} async-done(((bf16[4352,1088]{1,0:T(8,128)(2,1)}), bf16[544,1088]{1,0:T(8,128)(2,1)}) %reduce-scatter.49.cloned.1.call-update) | async-done | bytes 1183760 | tf_op jit(solution)/shard_map/reduce_scatter | solution.py:97
  2580.4 105.7 %reduce-scatter.47.cloned.1.call-done = bf16[544,1088]{1,0:T(8,128)(2,1)} async-done(((bf16[4352,1088]{1,0:T(8,128)(2,1)}), bf16[544,1088]{1,0:T(8,128)(2,1)}) %reduce-scatter.47.cloned.1.call-update) | async-done | bytes 1183760 | tf_op jit(solution)/shard_map/reduce_scatter | solution.py:97
  2693.8 93.1 %reduce-scatter.43.cloned.1.call-done = bf16[136,4352]{1,0:T(8,128)(2,1)} async-done(((bf16[1088,4352]{1,0:T(8,128)(2,1)}), bf16[136,4352]{1,0:T(8,128)(2,1)}) %reduce-scatter.43.cloned.1.call-update) | async-done | bytes 1183760 | tf_op jit(solution)/shard_map/reduce_scatter | solution.py:91
  2797.0 669.8 %while.71 = (s32[]{:T(128)}, f32[1,17,1024,64]{2,3,1,0:T(8,128)}, bf16[1,4096,2176]{1,2,0:T(8,128)(2,1)}, s32[1,4096]{1,0:T(1,128)}, s32[1,1024]{1,0:T(1,128)S(1...) while((s32[]{:T(128)}, f32[1,17,1024,64]{2,3,1,0:T(8,128)}, ...), condition=%wide.region_28.29_spmd.clone, body=%wide.region_27.28_spmd.clone.sunk | while | flops 5821170176 | bytes 205546800 | solution.py:422
  2816.0 22.1 fusion.296
  2899.4 22.2 fusion.296
  2984.0 22.2 fusion.296
  3068.0 22.0 fusion.296
  3487.9 140.3 %reduce-scatter.37.cloned.1.call-done = bf16[1,1024,2176]{1,2,0:T(8,128)(2,1)} async-done(((bf16[1,4096,2176]{1,2,0:T(8,128)(2,1)}), bf16[1,1024,2176]{1,2,0:T(8,128)(2,1)}) %reduce-scatter.37.cloned.1.call-update) | async-done | bytes 4456464 | tf_op jit(solution)/shard_map/reduce_scatter | solution.py:423
  3727.8 23.0 reduce-scatter.53.cloned.1.call-done
  3784.0 31.4 all-gather.51.cloned.1.call-done
  3884.2 34.0 all-reduce.41
  (965 shorter events, 2751.4 us)
Async XLA Ops:
  105.8 599.4 %all-gather.57.cloned.1.call-start = ((), (), s32[]{:S(2)}) async-start(), calls=%async_computation.28 | async-start | bytes 2820096 | tf_op jit(solution)/shard_map/all_gather | solution.py:32
  108.1 606.6 %all-gather.59.cloned.1.call-start = ((), (), s32[]{:S(2)}) async-start(), calls=%async_computation.29 | async-start | bytes 10653696 | tf_op jit(solution)/shard_map/all_gather | solution.py:36
  112.3 659.5 %all-gather.61.cloned.1.call-start = ((), (), s32[]{:S(2)}) async-start(), calls=%async_computation.30 | async-start | bytes 11280384 | tf_op jit(solution)/shard_map/all_gather | solution.py:38
  118.0 675.2 %all-gather.63.cloned.1.call-start = ((), (), s32[]{:S(2)}) async-start(), calls=%async_computation.31 | async-start | bytes 8146944 | tf_op jit(solution)/shard_map/all_gather | solution.py:29
  118.5 860.9 %all-gather.65.cloned.1.call-start = ((), (), s32[]{:S(2)}) async-start(), calls=%async_computation.32 | async-start | bytes 22282240 | tf_op jit(solution)/shard_map/all_gather | solution.py:283
  812.1 604.9 %all-gather.67.cloned.1.call-start = ((), (), s32[]{:S(2)}) async-start(), calls=%async_computation.33 | async-start | bytes 2820096 | tf_op jit(solution)/shard_map/all_gather | solution.py:32
  812.8 616.1 %all-gather.69.cloned.1.call-start = ((), (), s32[]{:S(2)}) async-start(), calls=%async_computation.34 | async-start | bytes 10653696 | tf_op jit(solution)/shard_map/all_gather | solution.py:36
  813.6 673.4 %all-gather.71.cloned.1.call-start = ((), (), s32[]{:S(2)}) async-start(), calls=%async_computation.35 | async-start | bytes 11280384 | tf_op jit(solution)/shard_map/all_gather | solution.py:38
  814.2 1557.9 %reduce-scatter.35.cloned.1.call-start = ((), (), s32[]{:S(2)}) async-start(), calls=%async_computation.16 | async-start | bytes 22282240 | tf_op jit(solution)/shard_map/reduce_scatter | solution.py:423
  2227.5 352.9 %reduce-scatter.49.cloned.1.call-start = ((), (), s32[]{:S(2)}) async-start(), calls=%async_computation.24 | async-start | bytes 11280384 | tf_op jit(solution)/shard_map/reduce_scatter | solution.py:97
  2246.9 439.2 %reduce-scatter.47.cloned.1.call-start = ((), (), s32[]{:S(2)}) async-start(), calls=%async_computation.22 | async-start | bytes 11280384 | tf_op jit(solution)/shard_map/reduce_scatter | solution.py:97
  2413.3 373.5 %reduce-scatter.43.cloned.1.call-start = ((), (), s32[]{:S(2)}) async-start(), calls=%async_computation.20 | async-start | bytes 10653696 | tf_op jit(solution)/shard_map/reduce_scatter | solution.py:91
  2459.7 1007.3 %reduce-scatter.65.cloned.1.call-start = ((), (), s32[]{:S(2)}) async-start(), calls=%async_computation.45 | async-start | bytes 2820096
  2466.6 1002.4 %reduce-scatter.61.cloned.1.call-start = ((), (), s32[]{:S(2)}) async-start(), calls=%async_computation.43 | async-start | bytes 2785280
  2478.3 992.8 %reduce-scatter.63.cloned.1.call-start = ((), (), s32[]{:S(2)}) async-start(), calls=%async_computation.44 | async-start | bytes 2820096
  2512.6 960.6 %reduce-scatter.41.cloned.1.call-start = ((), (), s32[]{:S(2)}) async-start(), calls=%async_computation.19 | async-start | bytes 8146944 | tf_op jit(solution)/shard_map/reduce_scatter | solution.py:70
  2527.0 950.1 %all-reduce.46.cloned.1.call-start = ((), (), s32[]{:S(2)}) async-start(), calls=%async_computation.46 | async-start | bytes 5013504
  2686.1 799.8 %reduce-scatter.59.cloned.1.call-start = ((), (), s32[]{:S(2)}) async-start(), calls=%async_computation.42 | async-start | bytes 2785280
  2790.5 837.8 %reduce-scatter.37.cloned.1.call-start = ((), (), s32[]{:S(2)}) async-start(), calls=%async_computation.17 | async-start | bytes 22282240 | tf_op jit(solution)/shard_map/reduce_scatter | solution.py:423
  3475.8 308.2 %all-gather.49.cloned.1.call-start = ((), (), s32[]{:S(2)}) async-start(), calls=%async_computation.23 | async-start | bytes 1740800 | tf_op jit(solution)/shard_map/all_gather | solution.py:142
  3479.4 336.0 %all-gather.51.cloned.1.call-start = ((), (), s32[]{:S(2)}) async-start(), calls=%async_computation.25 | async-start | bytes 1740800 | tf_op jit(solution)/shard_map/all_gather | solution.py:142
  3481.7 364.5 %all-gather.73.cloned.1.call-start = ((), (), s32[]{:S(2)}) async-start(), calls=%async_computation.36 | async-start | bytes 1566720 | tf_op jit(solution)/shard_map/all_gather | solution.py:139
  3487.9 468.7 %reduce-scatter.39.cloned.1.call-start = ((), (), s32[]{:S(2)}) async-start(), calls=%async_computation.18 | async-start | bytes 8146944 | tf_op jit(solution)/shard_map/reduce_scatter | solution.py:70
  3641.7 346.5 %reduce-scatter.51.cloned.1.call-start = ((), (), s32[]{:S(2)}) async-start(), calls=%async_computation.38 | async-start | bytes 2088960
  (177 other events, 5869.3 us)
Sparse Core Ops, SparseCore 0:
  11.2 76.8 all-gather.52
  105.9 165.8 all-gather.54
  273.5 32.8 all-gather.56
  308.5 90.0 all-gather.58
  400.7 94.0 all-gather.60
  496.3 70.9 all-gather.62
  812.2 167.2 all-gather.64
  981.1 32.8 all-gather.66
  1015.7 90.0 all-gather.68
  1107.8 94.0 all-gather.70
  2209.9 162.1 reduce-scatter.34
  2374.4 100.0 reduce-scatter.44
  2476.9 103.4 reduce-scatter.48
  2582.6 103.4 reduce-scatter.46
  2688.4 98.4 reduce-scatter.42
  2789.7 36.8 reduce-scatter.64
  2829.5 35.1 reduce-scatter.60
  2866.9 38.4 reduce-scatter.62
  2907.9 77.8 reduce-scatter.40
  2988.9 75.1 all-reduce.45
  3068.0 36.4 reduce-scatter.58
  3467.0 161.2 reduce-scatter.36
  3719.0 31.6 reduce-scatter.52
  3848.3 80.8 reduce-scatter.38
  (7 shorter events, 196.0 us)
where the time goes:
time: 4020 us; the launch traced here: 4010 us
  matrix products  2180 us (54%)
  waiting for transfers between devices  1020 us (25%)
  other arithmetic  466 us (12%)
  local copies, waits for them, and re-layouts  187 us (5%)
  blocking collectives  133 us (3%)
    dot_general x16, matrix products, back_visit(): jnp.einsum('sqhe,skhe->shqk', grad_heads, value_heads, preferred_element_...  352 us
    all_gather x2, waiting for transfers between devices, local(): lax.all_gather(key_local, 'ctx', axis=1, tiled=True)  309 us
    dot_general x16, matrix products, forward_block(): jnp.einsum('shqk,skhe->shqe', soft_part.astype(bf16), value_heads, prefer...  309 us
    dot_general x16, matrix products, back_visit(): jnp.einsum('shqk,sqhe->skhe', soft_low, grad_heads, preferred_element_typ...  272 us
    reduce_scatter x2, waiting for transfers between devices, local(): lax.psum_scatter(dkv_acc.astype(jnp.bfloat16), 'ctx', scatter_dimension=1...  263 us
    reduce_sum x16, other arithmetic, forward_block(): totals = totals * carried + jnp.sum(soft_part, axis=-1)  248 us
    dot_general x16, matrix products, forward_block(): jnp.einsum('sqhe,skhe->shqk', queries, key_heads, preferred_element_type=...  234 us
    dot_general x16, matrix products, back_visit(): jnp.einsum('sqhe,skhe->shqk', queries, key_heads, preferred_element_type=...  224 us
  transfers between devices with their start and end apart: 31, of which 17 were waited for; matrix products, arithmetic and copies ran while one was open for 51% of the time, Pallas kernels for 0%

commit v1 on v0

v1 whole, which is shorter than its diff:
```python
import functools
import jax, jax.numpy as jnp
from jax import lax
from jax.experimental import pallas as pl
from jax.experimental.pallas import tpu as pltpu
from jax.sharding import Mesh, PartitionSpec as P
f32=jnp.float32; bf16=jnp.bfloat16
NEG=-1e30
def dot_nt(a,b): return lax.dot_general(a,b,(((1,),(1,)),((),())),preferred_element_type=f32)
def dot_nn(a,b): return lax.dot_general(a,b,(((1,),(0,)),((),())),preferred_element_type=f32)

LOG2E=1.4426950408889634
def split(q,h,low):
    qs=q.astype(f32)*(0.125*LOG2E)
    hi=qs.astype(bf16).astype(f32); lo=qs-hi
    rl=pltpu.roll(lo,64,1)
    c=jnp.where(low,hi,rl) if h==0 else jnp.where(low,rl,hi)
    return c.astype(bf16)
def dup(k,h,low):
    kf=k.astype(f32); rl=pltpu.roll(kf,64,1)
    c=jnp.where(low,kf,rl) if h==0 else jnp.where(low,rl,kf)
    return c.astype(bf16)
def fwd_kernel(inv_ref, nb_ref, x_ref, o_ref, lse_ref, vt, kd, sb, acc, *, B, NB):
    s=pl.program_id(0)
    nb=nb_ref[s]
    lane=lax.broadcasted_iota(jnp.int32,(1,128),1)
    low=lane<64
    def tv(j,_):
        r=pl.multiple_of(inv_ref[s,j]*B,B)
        w=pl.multiple_of(j*B,B)
        t=x_ref[0,pl.ds(r,B),256:384].T
        one=(lax.broadcasted_iota(jnp.int32,(16,B),0)==0).astype(bf16)
        for h in range(2):
            vt[80*h:80*h+64,pl.ds(w,B)]=t[64*h:64*h+64,:]
            vt[80*h+64:80*h+80,pl.ds(w,B)]=one
            kd[h,pl.ds(w,B),:]=dup(x_ref[0,pl.ds(r,B),128:256],h,low)
        return 0
    lax.fori_loop(0,nb,tv,0)
    rr=lax.broadcasted_iota(jnp.int32,(B,B),0)
    cc=lax.broadcasted_iota(jnp.int32,(B,B),1)
    def qblock(i,_):
        r=pl.multiple_of(inv_ref[s,i]*B,B)
        q=x_ref[0,pl.ds(r,B),0:128]
        qh=[split(q,h,low) for h in range(2)]
        acc[...]=jnp.zeros_like(acc)
        def scores(j,slot):
            for h in range(2):
                sb[slot,h]=dot_nt(kd[h,pl.ds(pl.multiple_of(j*B,B),B),:],qh[h])
        def step(j,carry,diag):
            out=[]
            for h in range(2):
                m=carry[h]
                st=sb[j%2,h]
                if diag: st=jnp.where(rr<=cc,st,NEG)
                mn=jnp.maximum(m,jnp.max(st,axis=0,keepdims=True))
                p=jnp.exp2(st-mn)
                al=jnp.exp2(m-mn)
                v=vt[80*h:80*h+80,pl.ds(pl.multiple_of(j*B,B),B)]
                acc[h]=acc[h]*al+dot_nn(v,p.astype(bf16))
                out.append(mn)
            return tuple(out)
        scores(0,0)
        def both(j,c):
            scores(j+1,(j+1)%2)
            return step(j,c,False)
        n=jnp.full((1,B),NEG,f32)
        c=lax.fori_loop(0,i,both,(n,n))
        c=step(i,c,True)
        os=[]
        for h in range(2):
            l=acc[h,64:65,:]
            os.append(acc[h,0:64,:]*(1.0/l))
            lse_ref[0,pl.ds(h,1),pl.ds(r,B)]=c[h]+jnp.log2(l)
        o_ref[0,pl.ds(r,B),:]=jnp.concatenate(os,0).T.astype(bf16)
        return 0
    lax.fori_loop(0,nb,qblock,0)
    def pad(i,_):
        r=pl.multiple_of(inv_ref[s,i]*B,B)
        o_ref[0,pl.ds(r,B),:]=jnp.zeros((B,128),bf16)
        lse_ref[0,:,pl.ds(r,B)]=jnp.zeros((8,B),f32)
        return 0
    lax.fori_loop(nb,NB,pad,0)

def flash_fwd(x,inv,nb,B):
    S,N,_=x.shape
    NB=N//B
    return pl.pallas_call(functools.partial(fwd_kernel,B=B,NB=NB),
      out_shape=(jax.ShapeDtypeStruct((S,N,128),bf16),jax.ShapeDtypeStruct((S,8,N),f32)),
      grid_spec=pltpu.PrefetchScalarGridSpec(num_scalar_prefetch=2,grid=(S,),
        in_specs=[pl.BlockSpec((1,N,384),lambda s,*_:(s,0,0))],
        out_specs=[pl.BlockSpec((1,N,128),lambda s,*_:(s,0,0)),pl.BlockSpec((1,8,N),lambda s,*_:(s,0,0))],
        scratch_shapes=[pltpu.VMEM((160,N),bf16),pltpu.VMEM((2,N,128),bf16),pltpu.VMEM((2,2,B,B),f32),pltpu.VMEM((2,80,B),f32)]),
      compiler_params=pltpu.CompilerParams(vmem_limit_bytes=48<<20),
      cost_estimate=pl.CostEstimate(flops=S*4*N*N*128,bytes_accessed=S*N*1024,transcendentals=S*N*N),
      )(inv,nb,x)

def bwd_kernel(inv_ref, nb_ref, x_ref, o_ref, do_ref, lse_ref, dx_ref, kt, qd, dq, dk, dv, dl, *, B, NB):
    s=pl.program_id(0)
    nb=nb_ref[s]
    lane=lax.broadcasted_iota(jnp.int32,(1,128),1)
    low=lane<64
    hm=(lax.broadcasted_iota(jnp.int32,(8,128),1)//64==lax.broadcasted_iota(jnp.int32,(8,128),0)).astype(bf16)
    def prep(j,_):
        r=pl.multiple_of(inv_ref[s,j]*B,B)
        w=pl.multiple_of(j*B,B)
        kt[:,pl.ds(w,B)]=x_ref[0,pl.ds(r,B),128:256].T
        for h in range(2): qd[h,pl.ds(w,B),:]=split(x_ref[0,pl.ds(r,B),0:128],h,low)
        prod=o_ref[0,pl.ds(r,B),:].astype(f32)*do_ref[0,pl.ds(r,B),:].astype(f32)
        hi=prod.astype(bf16); lo=(prod-hi.astype(f32)).astype(bf16)
        dl[:,pl.ds(w,B)]=dot_nt(hm,hi)+dot_nt(hm,lo)
        dq[:,pl.ds(w,B)]=jnp.zeros((128,B),f32)
        return 0
    lax.fori_loop(0,nb,prep,0)
    rr=lax.broadcasted_iota(jnp.int32,(B,B),0)
    cc=lax.broadcasted_iota(jnp.int32,(B,B),1)
    def kblock(j,_):
        r=pl.multiple_of(inv_ref[s,j]*B,B)
        k=x_ref[0,pl.ds(r,B),128:256]
        v=x_ref[0,pl.ds(r,B),256:384]
        kdh=[dup(k,h,low) for h in range(2)]
        dk[...]=jnp.zeros_like(dk); dv[...]=jnp.zeros_like(dv)
        def step(i,diag):
            ri=pl.multiple_of(inv_ref[s,i]*B,B)
            wi=pl.multiple_of(i*B,B)
            q=x_ref[0,pl.ds(ri,B),0:128]*jnp.asarray(0.125,bf16)
            do=do_ref[0,pl.ds(ri,B),:]
            zero=jnp.zeros_like(q)
            dvs=[];dks=[]
            for h in range(2):
                qh=jnp.where(low,q,zero) if h==0 else jnp.where(low,zero,q)
                doh=jnp.where(low,do,zero) if h==0 else jnp.where(low,zero,do)
                st=dot_nt(kdh[h],qd[h,pl.ds(wi,B),:])
                p=jnp.exp2(st-lse_ref[0,pl.ds(h,1),pl.ds(ri,B)])
                if diag: p=jnp.where(rr<=cc,p,0.0)
                dvs.append(dot_nn(p.astype(bf16),doh))
                dp=dot_nt(v,doh)
                ds=(p*(dp-dl[pl.ds(h,1),pl.ds(wi,B)])).astype(bf16)
                dks.append(dot_nn(ds,qh))
                kh=kt[64*h:64*h+64,pl.ds(pl.multiple_of(j*B,B),B)]
                dq[64*h:64*h+64,pl.ds(wi,B)]+=dot_nn(kh,ds)
            dv[...]+=dvs[0]+dvs[1]
            dk[...]+=dks[0]+dks[1]
        step(j,True)
        def body(i,_):
            step(i,False); return 0
        lax.fori_loop(j+1,nb,body,0)
        dx_ref[0,pl.ds(r,B),128:256]=dk[...].astype(bf16)
        dx_ref[0,pl.ds(r,B),256:384]=dv[...].astype(bf16)
        return 0
    lax.fori_loop(0,nb,kblock,0)
    def fin(i,_):
        r=pl.multiple_of(inv_ref[s,i]*B,B)
        dx_ref[0,pl.ds(r,B),0:128]=(dq[:,pl.ds(pl.multiple_of(i*B,B),B)].T*0.125).astype(bf16)
        return 0
    lax.fori_loop(0,nb,fin,0)
    def pad(i,_):
        r=pl.multiple_of(inv_ref[s,i]*B,B)
        dx_ref[0,pl.ds(r,B),:]=jnp.zeros((B,384),bf16)
        return 0
    lax.fori_loop(nb,NB,pad,0)

def flash_bwd(x,o,do,lse,inv,nb,B):
    S,N,_=x.shape
    NB=N//B
    return pl.pallas_call(functools.partial(bwd_kernel,B=B,NB=NB),
      out_shape=jax.ShapeDtypeStruct((S,N,384),bf16),
      grid_spec=pltpu.PrefetchScalarGridSpec(num_scalar_prefetch=2,grid=(S,),
        in_specs=[pl.BlockSpec((1,N,384),lambda s,*_:(s,0,0)),pl.BlockSpec((1,N,128),lambda s,*_:(s,0,0)),
                  pl.BlockSpec((1,N,128),lambda s,*_:(s,0,0)),pl.BlockSpec((1,8,N),lambda s,*_:(s,0,0))],
        out_specs=pl.BlockSpec((1,N,384),lambda s,*_:(s,0,0)),
        scratch_shapes=[pltpu.VMEM((128,N),bf16),pltpu.VMEM((2,N,128),bf16),pltpu.VMEM((128,N),f32),pltpu.VMEM((B,128),f32),pltpu.VMEM((B,128),f32),pltpu.VMEM((8,N),f32)]),
      compiler_params=pltpu.CompilerParams(vmem_limit_bytes=48<<20),
      cost_estimate=pl.CostEstimate(flops=S*10*N*N*128,bytes_accessed=S*N*2400,transcendentals=S*N*N),
      )(inv,nb,x,o,do,lse)


def one_fwd_kernel(own_ref, q_ref, x_ref, o_ref, lse_ref, vt, sb, acc, *, B, NB):
    nb = own_ref[NB + 2]
    def tv(j,_):
        r=pl.multiple_of(own_ref[j]*B,B)
        t=x_ref[pl.ds(r,B),:].T
        w=pl.multiple_of(j*B,B)
        vt[0:64,pl.ds(w,B)]=t[64:128,:]
        vt[64:80,pl.ds(w,B)]=(lax.broadcasted_iota(jnp.int32,(16,B),0)==0).astype(bf16)
        return 0
    lax.fori_loop(0,nb,tv,0)
    rr=lax.broadcasted_iota(jnp.int32,(B,B),0)
    cc=lax.broadcasted_iota(jnp.int32,(B,B),1)
    for t in range(2):
        i=own_ref[NB+t]
        @pl.when(i>=nb)
        def _():
            o_ref[t*B:(t+1)*B,:]=jnp.zeros((B,64),bf16)
            lse_ref[:,t*B:(t+1)*B]=jnp.zeros((8,B),f32)
        @pl.when(i<nb)
        def _():
            qs=q_ref[t*B:(t+1)*B,:].astype(f32)*(0.125*LOG2E)
            q=qs.astype(bf16)
            ql=(qs-q.astype(f32)).astype(bf16)
            acc[...]=jnp.zeros_like(acc)
            def step(j,m,diag):
                k=x_ref[pl.ds(pl.multiple_of(own_ref[j]*B,B),B),0:64]
                st=dot_nt(k,q)+dot_nt(k,ql)
                if diag: st=jnp.where(rr<=cc,st,NEG)
                mn=jnp.maximum(m,jnp.max(st,axis=0,keepdims=True))
                p=jnp.exp2(st-mn)
                al=jnp.exp2(m-mn)
                v=vt[:,pl.ds(pl.multiple_of(j*B,B),B)]
                acc[...]=acc[...]*al+dot_nn(v,p.astype(bf16))
                return mn
            m=lax.fori_loop(0,i,lambda j,m: step(j,m,False),jnp.full((1,B),NEG,f32))
            m=step(i,m,True)
            l=acc[64:65,:]
            o_ref[t*B:(t+1)*B,:]=(acc[0:64,:]*(1.0/l)).T.astype(bf16)
            lse_ref[:,t*B:(t+1)*B]=jnp.broadcast_to(m+jnp.log2(l),(8,B))


def one_fwd(q,x,own,B):
    N=x.shape[0]; R=q.shape[0]; NB=N//B
    full=lambda *_:(0,0)
    return pl.pallas_call(functools.partial(one_fwd_kernel,B=B,NB=NB),
      out_shape=(jax.ShapeDtypeStruct((R,64),bf16),jax.ShapeDtypeStruct((8,R),f32)),
      grid_spec=pltpu.PrefetchScalarGridSpec(num_scalar_prefetch=1,grid=(1,),
        in_specs=[pl.BlockSpec((R,64),full),pl.BlockSpec((N,128),full)],
        out_specs=[pl.BlockSpec((R,64),full),pl.BlockSpec((8,R),full)],
        scratch_shapes=[pltpu.VMEM((80,N),bf16),pltpu.VMEM((B,B),f32),pltpu.VMEM((80,B),f32)]),
      compiler_params=pltpu.CompilerParams(vmem_limit_bytes=48<<20),
      cost_estimate=pl.CostEstimate(flops=4*R*N*128,bytes_accessed=N*256+R*512,transcendentals=R*N),
      )(own,q,x)


def one_bwd_kernel(own_ref, q_ref, x_ref, o_ref, do_ref, lse_ref, dq_ref, dx_ref, dkv, dq, *, B, NB):
    nb = own_ref[NB + 2]
    rr=lax.broadcasted_iota(jnp.int32,(B,B),0)
    cc=lax.broadcasted_iota(jnp.int32,(B,B),1)
    ones=jnp.ones((8,64),bf16)
    dkv[...]=jnp.zeros_like(dkv)
    for t in range(2):
        i=own_ref[NB+t]
        sl=slice(t*B,(t+1)*B)
        @pl.when(i>=nb)
        def _():
            dq_ref[sl,:]=jnp.zeros((B,64),bf16)
        @pl.when(i<nb)
        def _():
            qr=q_ref[sl,:]
            qs=qr.astype(f32)*(0.125*LOG2E)
            q=qs.astype(bf16)
            ql=(qs-q.astype(f32)).astype(bf16)
            qd=qr*jnp.asarray(0.125,bf16)
            do=do_ref[sl,:]
            prod=o_ref[sl,:].astype(f32)*do.astype(f32)
            hi=prod.astype(bf16); lo=(prod-hi.astype(f32)).astype(bf16)
            dl=(dot_nt(ones,hi)+dot_nt(ones,lo))[0:1,:]
            lse=lse_ref[0:1,sl]
            dq[...]=jnp.zeros_like(dq)
            def step(j,diag):
                r=pl.multiple_of(own_ref[j]*B,B)
                k=x_ref[pl.ds(r,B),0:64]
                v=x_ref[pl.ds(r,B),64:128]
                st=dot_nt(k,q)+dot_nt(k,ql)
                p=jnp.exp2(st-lse)
                if diag: p=jnp.where(rr<=cc,p,0.0)
                dp=dot_nt(v,do)
                ds=(p*(dp-dl)).astype(bf16)
                dkv[pl.ds(r,B),64:128]+=dot_nn(p.astype(bf16),do)
                dkv[pl.ds(r,B),0:64]+=dot_nn(ds,qd)
                dq[...]+=dot_nn(k.T,ds)
            def body(j,_):
                step(j,False); return 0
            lax.fori_loop(0,i,body,0)
            step(i,True)
            dq_ref[sl,:]=(dq[...].T*0.125).astype(bf16)
    dx_ref[...]=dkv[...].astype(bf16)


def one_bwd(q,x,o,do,lse,own,B):
    N=x.shape[0]; R=q.shape[0]; NB=N//B
    full=lambda *_:(0,0)
    return pl.pallas_call(functools.partial(one_bwd_kernel,B=B,NB=NB),
      out_shape=(jax.ShapeDtypeStruct((R,64),bf16),jax.ShapeDtypeStruct((N,128),bf16)),
      grid_spec=pltpu.PrefetchScalarGridSpec(num_scalar_prefetch=1,grid=(1,),
        in_specs=[pl.BlockSpec((R,64),full),pl.BlockSpec((N,128),full),pl.BlockSpec((R,64),full),pl.BlockSpec((R,64),full),pl.BlockSpec((8,R),full)],
        out_specs=[pl.BlockSpec((R,64),full),pl.BlockSpec((N,128),full)],
        scratch_shapes=[pltpu.VMEM((N,128),f32),pltpu.VMEM((64,B),f32)]),
      compiler_params=pltpu.CompilerParams(vmem_limit_bytes=48<<20),
      cost_estimate=pl.CostEstimate(flops=10*R*N*128,bytes_accessed=N*512+R*1024,transcendentals=R*N),
      )(own,q,x,o,do,lse)


HEADS = 17
EPSILON = 1e-05
FS = ("zz", "core")


def norm_parts(v):
    mean = jnp.mean(v, axis=-1, keepdims=True)
    c = v - mean
    r = lax.rsqrt(jnp.mean(c * c, axis=-1, keepdims=True) + EPSILON)
    return c * r, r


def norm_back(dn, v, gain):
    xhat, r = norm_parts(v)
    y = dn * gain
    a = jnp.mean(y, axis=-1, keepdims=True)
    b = jnp.mean(y * xhat, axis=-1, keepdims=True)
    return r * (y - a - xhat * b), jnp.sum(dn * xhat, axis=0), jnp.sum(dn, axis=0)


def gelu_parts(u):
    z = jnp.abs(u) * 0.7071067811865476
    t = 1.0 / (1.0 + 0.3275911 * z)
    e = jnp.exp(-z * z)
    poly = t * (0.254829592 + t * (-0.284496736 + t * (1.421413741 + t * (-1.453152027 + t * 1.061405429))))
    half = 0.5 * poly * e
    cdf = jnp.where(u >= 0, 1.0 - half, half)
    return u * cdf, cdf + u * e * 0.3989422804014327


def local(
    tokens, cotangent, lengths, block_order,
    ln1_gain, ln1_bias, qkv_weight, q_bias, v_bias, out_weight, out_bias,
    ln2_gain, ln2_bias, up_weight, up_bias, down_weight, down_bias,
    *, G, S,
):
    slots, rows, width = tokens.shape
    C = lax.axis_size("ctx")
    me = lax.axis_index("ctx")
    group = ("core", "ctx") if S == 2 else ("ctx",)
    N = rows * C
    B = rows // 2
    NB = 2 * C
    L = ln1_gain.shape[0]
    shard = ln1_gain.shape[1]
    HW = G * 128
    x_tokens = tokens[0]

    steps = jnp.arange(NB, dtype=jnp.int32)
    order = block_order[0]
    inverse = jnp.sum(jnp.where(order[None, :] == steps[:, None], steps[None, :], 0), axis=1).astype(jnp.int32)
    count = (lengths + (B - 1)) // B
    meta = jnp.concatenate([inverse, count])
    both = lax.all_gather(meta, "core") if S == 2 else meta[None]
    inv, nb = both[:, :NB], both[:, NB]
    own = jnp.concatenate([inverse, lax.dynamic_slice_in_dim(order, 2 * me, 2, 0), count])
    own_pos = (lax.dynamic_slice_in_dim(order, 2 * me, 2, 0)[:, None] * B + jnp.arange(B, dtype=jnp.int32)).reshape(rows, 1)
    live = (own_pos < lengths[0]).astype(f32)

    vectors = [ln1_gain, ln1_bias, q_bias, v_bias, out_bias, ln2_gain, ln2_bias, down_bias, up_bias]
    vec = jnp.concatenate(vectors, axis=1).astype(bf16)
    vec = lax.all_gather(vec, FS).astype(f32)

    def vector(index, layer):
        if index < 8:
            return vec[:, layer, index * shard:(index + 1) * shard].reshape(-1)
        return vec[:, layer, 8 * shard:].reshape(-1)

    def pack(w):
        n = w.shape[0]
        w = w.reshape(n, 3, HEADS, 64)
        main = w[:, :, :16].reshape(n, 3, G, 128)
        main = jnp.transpose(main, (0, 2, 1, 3)).reshape(n, G * 384)
        tail = jnp.stack([w[:, 1, 16], w[:, 2, 16], w[:, 0, 16]], axis=1).reshape(n, 192)
        return jnp.concatenate([main, tail], axis=1)

    def unpack(w):
        n = w.shape[0]
        main = jnp.transpose(w[:, :G * 384].reshape(n, G, 3, 128), (0, 2, 1, 3)).reshape(n, 3, 1024)
        tail = w[:, G * 384:].reshape(n, 3, 64)
        tail = jnp.stack([tail[:, 2], tail[:, 0], tail[:, 1]], axis=1)
        return jnp.concatenate([main, tail], axis=2).reshape(n, 3 * width)

    def fetch(w):
        return lax.all_gather(w.astype(bf16), FS, axis=0, tiled=True)

    weights = []
    for layer in range(L):
        weights.append((
            fetch(pack(qkv_weight[layer].astype(bf16))),
            fetch(out_weight[layer]),
            fetch(up_weight[layer]),
            fetch(down_weight[layer]),
        ))

    def exchange(x):
        return lax.all_to_all(x, group, 0, 0)

    stream = x_tokens.astype(f32)
    records = []
    for layer in range(L):
        qkv_w, out_w, up_w, down_w = weights[layer]
        xhat, _ = norm_parts(stream)
        n1 = (xhat * vector(0, layer) + vector(1, layer)).astype(bf16)
        q_b, v_b = vector(2, layer), vector(3, layer)
        bias = pack(jnp.concatenate([q_b, jnp.zeros_like(q_b), v_b])[None])[0]
        wide = jnp.einsum("rd,dgc->grc", n1, qkv_w[:, :G * 384].reshape(width, G, 384), preferred_element_type=f32)
        wide = (wide + bias[:G * 384].reshape(G, 1, 384)).astype(bf16)
        tail = (jnp.dot(n1, qkv_w[:, G * 384:], preferred_element_type=f32) + bias[G * 384:]).astype(bf16)
        kv16 = lax.all_gather(tail[:, :128], "ctx", axis=0, tiled=True)
        q16 = tail[:, 128:]
        heads = exchange(wide).reshape(S, N, 384)
        o, lse = flash_fwd(heads, inv, nb, B)
        o16, lse16 = one_fwd(q16, kv16, own, B)
        o_back = exchange(o.reshape(G, rows, 128))
        mixed = jnp.concatenate([jnp.transpose(o_back, (1, 0, 2)).reshape(rows, HW), o16], axis=1)
        m = stream + jnp.dot(mixed, out_w, preferred_element_type=f32) + vector(4, layer)
        xhat2, _ = norm_parts(m)
        n2 = (xhat2 * vector(5, layer) + vector(6, layer)).astype(bf16)
        u = jnp.dot(n2, up_w, preferred_element_type=f32) + vector(8, layer)
        a, slope = gelu_parts(u)
        a = a.astype(bf16)
        slope = slope.astype(bf16)
        records.append((stream, n1, heads, kv16, q16, o, lse, o16, lse16, mixed, m, n2, a, slope))
        stream = m + jnp.dot(a, down_w, preferred_element_type=f32) + vector(7, layer)
    activations = (stream * live).astype(bf16)[None]

    def reduce_fsdp(g):
        return lax.psum_scatter(g.astype(bf16), FS, scatter_dimension=0, tiled=True)

    def reduce_ctx(g):
        t = lax.psum_scatter(g, "ctx", scatter_dimension=0, tiled=True)
        return lax.all_gather(t, "ctx", axis=0, tiled=True).astype(f32)

    grad = cotangent[0].astype(f32) * live
    matrices = [None] * L
    small = [None] * L
    for layer in reversed(range(L)):
        stream_in, n1, heads, kv16, q16, o, lse, o16, lse16, mixed, m, n2, a, slope = records[layer]
        qkv_w, out_w, up_w, down_w = weights[layer]
        gb = grad.astype(bf16)
        d_down_b = jnp.sum(gb.astype(f32), axis=0)
        d_down = reduce_fsdp(jnp.einsum("rf,rd->fd", a, gb, preferred_element_type=f32))
        du = (jnp.einsum("rd,fd->rf", gb, down_w, preferred_element_type=f32) * slope.astype(f32)).astype(bf16)
        d_up_b = jnp.sum(du.astype(f32), axis=0)
        d_up = reduce_fsdp(jnp.einsum("rd,rf->df", n2, du, preferred_element_type=f32))
        dn2 = jnp.einsum("rf,df->rd", du, up_w, preferred_element_type=f32)
        back, d_gain2, d_bias2 = norm_back(dn2, m, vector(5, layer))
        gm = grad + back
        gmb = gm.astype(bf16)
        d_out_b = jnp.sum(gmb.astype(f32), axis=0)
        d_out = reduce_fsdp(jnp.einsum("rd,re->de", mixed, gmb, preferred_element_type=f32))
        d_o = jnp.einsum("re,gce->grc", gmb, out_w[:HW].reshape(G, 128, width), preferred_element_type=f32).astype(bf16)
        d_o16 = jnp.einsum("re,ce->rc", gmb, out_w[HW:], preferred_element_type=f32).astype(bf16)
        d_oh = exchange(d_o).reshape(S, N, 128)
        d_heads = flash_bwd(heads, o, d_oh, lse, inv, nb, B)
        dq16, dkv16 = one_bwd(q16, kv16, o16, d_o16, lse16, own, B)
        dkv16 = lax.psum_scatter(dkv16, "ctx", scatter_dimension=0, tiled=True)
        d_wide = exchange(d_heads.reshape(G, rows, 384))
        d_tail = jnp.concatenate([dkv16.astype(bf16), dq16], axis=1)
        d_row = jnp.concatenate([jnp.transpose(d_wide, (1, 0, 2)).reshape(rows, G * 384), d_tail], axis=1)
        d_qkv = reduce_fsdp(jnp.einsum("rd,rc->dc", n1, d_row, preferred_element_type=f32))
        sums = unpack(jnp.sum(d_row.astype(f32), axis=0)[None])[0]
        dn1 = jnp.einsum("rc,dc->rd", d_row, qkv_w, preferred_element_type=f32)
        back, d_gain1, d_bias1 = norm_back(dn1, stream_in, vector(0, layer))
        grad = gm + back
        parts = [jnp.transpose(d_qkv.reshape(shard, 3, width), (1, 0, 2)).reshape(3 * shard, width), d_out,
                 jnp.transpose(d_up.reshape(shard, 4, width), (1, 0, 2)).reshape(4 * shard, width), d_down]
        matrices[layer] = reduce_ctx(jnp.concatenate(parts, axis=0))
        small[layer] = jnp.concatenate([
            t.reshape(-1, n) for t, n in (
                (d_gain1, shard), (d_bias1, shard), (sums[:width], shard), (sums[2 * width:], shard), (d_out_b, shard),
                (d_gain2, shard), (d_bias2, shard), (d_down_b, shard), (d_up_b, 4 * shard))], axis=1)

    vec_grads = jnp.stack(small, axis=1)
    vec_grads = lax.psum_scatter(vec_grads, FS, scatter_dimension=0, tiled=True)
    vec_grads = lax.psum(vec_grads, "ctx")[0]
    vg = [vec_grads[:, i * shard:(i + 1) * shard] for i in range(8)] + [vec_grads[:, 8 * shard:]]

    def take(layer, start, cols):
        t = matrices[layer][start * shard:(start + cols) * shard]
        return jnp.transpose(t.reshape(cols, shard, width), (1, 0, 2)).reshape(shard, cols * width)

    g_qkv = jnp.stack([unpack(take(layer, 0, 3)) for layer in range(L)])
    g_out = jnp.stack([take(layer, 3, 1) for layer in range(L)])
    g_up = jnp.stack([take(layer, 4, 4) for layer in range(L)])
    g_down = jnp.stack([matrices[layer][8 * shard:] for layer in range(L)])
    return (activations, grad[None], vg[0], vg[1], g_qkv, vg[2], vg[3], g_out, vg[4], vg[5], vg[6], g_up, vg[8], g_down, vg[7])


def solution(mesh):
    F, C = mesh.devices.shape
    inner = Mesh(mesh.devices.reshape(F // 2, 2, C), ("zz", "core", "ctx"))
    S = 2 if 16 // (2 * C) >= 2 else 1
    G = S * C
    rows = P(FS, "ctx", None)
    vec, mat = P(None, FS), P(None, FS, None)
    return jax.shard_map(
        functools.partial(local, G=G, S=S),
        mesh=inner,
        in_specs=(rows, rows, P(FS), P(FS, None), vec, vec, mat, vec, vec, mat, vec, vec, vec, mat, vec, mat, vec),
        out_specs=(rows, rows, vec, vec, mat, vec, vec, mat, vec, vec, vec, mat, vec, mat, vec),
        check_vma=False,
    )
```

time: 4020 us -> 2070 us (0.51)
  matrix products: 2180 us -> 404 us
  other arithmetic: 466 us -> 83.8 us
  Pallas kernels: 0 us -> 125 us
  blocking collectives: 133 us -> 177 us
    dot_general x136 -> x28, matrix products: 2180 us -> 404 us  [the longest x2 71.9 us: local(): u = jnp.dot(n2, up_w, preferred_element_type=f32) + vector(8, layer)]
    reduce_sum x32 -> x11, other arithmetic: 284 us -> 34.9 us  [the longest x2 11 us: local(): d_out_b = jnp.sum(gmb.astype(f32), axis=0)]
    all_gather x14 -> x12, waiting for transfers between devices: 426 us -> 245 us  [the longest x8 187 us: fetch(): return lax.all_gather(w.astype(bf16), FS, axis=0, tiled=True)]
    all_to_all x0 -> x5, waiting for transfers between devices: none -> 169 us  [exchange(): return lax.all_to_all(x, group, 0, 0)]
    all_to_all x0 -> x3, blocking collectives: none -> 143 us  [exchange(): return lax.all_to_all(x, group, 0, 0)]
    pallas_call x0 -> x8, Pallas kernels: none -> 125 us  [the longest x2 65.7 us: flash_bwd(): pl.pallas_call(functools.partial(bwd_kernel, B=B, NB=NB), out_shape=jax.S...]
    all_gather x5 -> x1, blocking collectives: 83.2 us -> 15.7 us  [local(): vec = lax.all_gather(vec, FS).astype(f32)]
    unnamed x40 -> x30, waiting for transfers between devices: 70.9 us -> 136 us
  transfers between devices with their start and end apart: 31 -> 30, of which waited for: 17 -> 19; matrix products, arithmetic and copies ran while one was open for 51% -> 21% of each run, Pallas kernels for 0% -> 4%
where the time goes in v1:
time: 2070 us; the launch traced here: 2060 us
  waiting for transfers between devices  1030 us (50%)
  matrix products  404 us (20%)
  local copies, waits for them, and re-layouts  195 us (9%)
  blocking collectives  177 us (9%)
  Pallas kernels  125 us (6%)
  other arithmetic  83.8 us (4%)
  starting transfers between devices  25 us (1%)
    reduce_scatter x6, waiting for transfers between devices, reduce_fsdp(): return lax.psum_scatter(g.astype(bf16), FS, scatter_dimension=0, tiled=True)  378 us
    all_gather x8, waiting for transfers between devices, fetch(): return lax.all_gather(w.astype(bf16), FS, axis=0, tiled=True)  187 us
    all_to_all x5, waiting for transfers between devices, exchange(): return lax.all_to_all(x, group, 0, 0)  169 us
    all_to_all x3, blocking collectives, exchange(): return lax.all_to_all(x, group, 0, 0)  143 us
    unnamed x30, waiting for transfers between devices  136 us
    reduce_scatter x2, waiting for transfers between devices, local(): dkv16 = lax.psum_scatter(dkv16, 'ctx', scatter_dimension=0, tiled=True)  106 us
    dot_general x2, matrix products, local(): u = jnp.dot(n2, up_w, preferred_element_type=f32) + vector(8, layer)  71.9 us
    pallas_call x2, Pallas kernels, flash_bwd(): pl.pallas_call(functools.partial(bwd_kernel, B=B, NB=NB), out_shape=jax.S...  65.7 us
  transfers between devices with their start and end apart: 30, of which 19 were waited for; matrix products, arithmetic and copies ran while one was open for 21% of the time, Pallas kernels for 4%

profile of v1, /device:TPU:0, one launch (start us, length us, event | category | flops | bytes accessed | tf_op | source)
XLA Modules:
  0.0 2063.3 jit_solution(1563731830458750793)
XLA Ops:
  41.8 54.4 %all-gather.20.cloned.1.call-done = bf16[1088,3264]{1,0:T(8,128)(2,1)} async-done(((bf16[136,3264]{1,0:T(8,128)(2,1)}), bf16[1088,3264]{1,0:T(8,128)(2,1)}) %all-gather.20.cloned.1.call-update) | async-done | bytes 7102480 | tf_op jit(solution)/shard_map/all_gather | solution.py:375
  145.1 65.6 %all-to-all-done = bf16[8,1024,384]{1,2,0:T(8,128)(2,1)} async-done(((bf16[8,1024,384]{1,2,0:T(8,128)(2,1)}), bf16[8,1024,384]{1,2,0:T(8,128)(2,1)}, u32[]{:S(2)}, u32[]{:S(2)}) %all-to-all-start) | async-done | bytes 6291488 | tf_op jit(solution)/shard_map/all_to_all | solution.py:387
  283.2 35.3 %multiply_convert_fusion.3 = (bf16[1024,4352]{1,0:T(8,128)(2,1)}, f32[1024,4352]{1,0:T(8,128)}) fusion(f32[4352]{0:T(1024)S(1)} %add.320, bf16[1,1088,4352]{2,1,0:T(8,128)(2,1)} %all-gather.34.cloned.1.call-done, f32[1024,1088]{0,1:T(8,128)} %copy-done.27, f32[1088]{0:T(1024)S(1)} %add.317, f32[1088]{0:T(1024)S(1)} %mul.344, f32[1024]{0:T(1024)S(1)} %add_rsqrt_fusion.2, ...), kind=kOutput, calls=%fused_computation.17 | convolution fusion | flops 9809756160 | bytes 40699392 | tf_op jit(solution)/shard_map/dot_general | solution.py:410
  318.6 29.8 %all-gather.36.cloned.1.call-done = bf16[1,4352,1088]{2,1,0:T(8,128)(2,1)} async-done(((bf16[1,544,1088]{2,1,0:T(8,128)(2,1)}), bf16[1,4352,1088]{2,1,0:T(8,128)(2,1)}) %all-gather.36.cloned.1.call-update) | async-done | bytes 9469968 | tf_op jit(solution)/shard_map/all_gather | solution.py:375
  371.9 49.6 %all-gather.24.cloned.1.call-done = bf16[1088,3264]{1,0:T(8,128)(2,1)} async-done(((bf16[136,3264]{1,0:T(8,128)(2,1)}), bf16[1088,3264]{1,0:T(8,128)(2,1)}) %all-gather.24.cloned.1.call-update) | async-done | bytes 7102480 | tf_op jit(solution)/shard_map/all_gather | solution.py:375
  440.1 83.3 %all_to_all.40 = bf16[8,1024,384]{1,2,0:T(8,128)(2,1)} all-to-all(bf16[8,1024,384]{1,2,0:T(8,128)(2,1)S(1)} %fusion.23), channel_id=1, replica_groups=mesh['zz'=4,'core'=2,'ctx'=4] {'core','ctx'}, dimensions={0} | all-to-all | bytes 12582912 | tf_op jit(solution)/shard_map/all_to_all | solution.py:387
  599.1 36.6 %multiply_convert_fusion.2 = (bf16[1024,4352]{1,0:T(8,128)(2,1)}, f32[1024,4352]{1,0:T(8,128)}) fusion(f32[4352]{0:T(1024)S(1)} %add.350, bf16[1,1088,4352]{2,1,0:T(8,128)(2,1)} %all-gather.40.cloned.1.call-done, f32[1024,1088]{0,1:T(8,128)} %copy-done.20, f32[1088]{0:T(1024)S(1)} %add.347, f32[1088]{0:T(1024)S(1)} %mul.368, f32[1024]{0:T(1024)S(1)} %add_rsqrt_fusion, ...), kind=kOutput, calls=%fused_computation.16 | convolution fusion | flops 9809756160 | bytes 40699392 | tf_op jit(solution)/shard_map/dot_general | solution.py:410
  635.7 52.7 %all-gather.42.cloned.1.call-done = bf16[1,4352,1088]{2,1,0:T(8,128)(2,1)} async-done(((bf16[1,544,1088]{2,1,0:T(8,128)(2,1)}), bf16[1,4352,1088]{2,1,0:T(8,128)(2,1)}) %all-gather.42.cloned.1.call-update) | async-done | bytes 9469968 | tf_op jit(solution)/shard_map/all_gather | solution.py:375
  688.4 34.5 %convert_reduce_fusion = (f32[4352]{0:T(1024)}, bf16[1024,4352]{1,0:T(8,128)(2,1)}) fusion(f32[1024,4352]{1,0:T(8,128)} %get-tuple-element.124, f32[4352]{0:T(1024)S(1)} %add.350, bf16[1,4352,1088]{2,1,0:T(8,128)(2,1)} %all-gather.42.cloned.1.call-done, bf16[1,1024,1088]{1,2,0:T(8,128)(2,1)} %param.18, f32[1024]{0:T(1024)S(1)} %bitcast.376), kind=kOutput, calls=%fused_computation.10 | convolution fusion | flops 9838718976 | bytes 38475776 | tf_op jit(solution)/shard_map/rd,fd->rf/dot_general | solution.py:434
  749.7 29.7 %all_to_all.41 = bf16[8,1024,128]{2,1,0:T(8,128)(2,1)S(1)} all-to-all(bf16[8,1024,128]{2,1,0:T(8,128)(2,1)S(1)} %convert_bitcast_fusion.2), channel_id=1, replica_groups=mesh['zz'=4,'core'=2,'ctx'=4] {'core','ctx'}, dimensions={0} | all-to-all | bytes 4194304 | tf_op jit(solution)/shard_map/all_to_all | solution.py:387
  779.4 32.8 %shard_map.284 = bf16[2,4096,384]{2,1,0:T(8,128)(2,1)} custom-call(s32[2,8]{1,0:T(2,128)S(1)} %bitcast.332, s32[2]{0:T(128)S(1)} %copy-done.16, bf16[2,4096,384]{2,1,0:T(8,128)(2,1)} %bitcast.351, bf16[2,4096,128]{2,1,0:T(8,128)(2,1)S(1)} %copy-done.1, bf16[2,4096,128]{2,1,0:T(8,128)(2,1)S(1)} %bitcast.329, f32[2,8,4096]{2,1,0:T(8,128)S(1)} %get-tuple-element.31.lse_ref), custom_call_target="tpu_custom_call" | custom-call | flops 42949672960 | bytes 19660800 | tf_op jit(solution)/shard_map/pallas_call | solution.py:165
  835.2 105.5 %reduce-scatter.21.cloned.1.call-done = bf16[1024,128]{1,0:T(8,128)(2,1)} async-done(((bf16[4096,128]{1,0:T(8,128)(2,1)}), bf16[1024,128]{1,0:T(8,128)(2,1)}) %reduce-scatter.21.cloned.1.call-update) | async-done | bytes 262160 | tf_op jit(solution)/shard_map/reduce_scatter | solution.py:448
  966.4 30.9 %convert_reduce_fusion.1 = (f32[4352]{0:T(1024)}, bf16[1024,4352]{1,0:T(8,128)(2,1)}) fusion(f32[1024,4352]{1,0:T(8,128)} %get-tuple-element.118, f32[4352]{0:T(1024)S(1)} %copy-done.90, bf16[1,4352,1088]{2,1,0:T(8,128)(2,1)} %all-gather.36.cloned.1.call-done, f32[1024,1088]{0,1:T(8,128)S(1)} %get-tuple-element.78), kind=kOutput, calls=%fused_computation.11 | convolution fusion | flops 9836490752 | bytes 40699904 | tf_op jit(solution)/shard_map/rd,fd->rf/dot_general | solution.py:434
  1114.8 30.1 %all_to_all.42 = bf16[8,1024,128]{2,1,0:T(8,128)(2,1)S(1)} all-to-all(bf16[8,1024,128]{2,1,0:T(8,128)(2,1)S(1)} %convert_bitcast_fusion.1), channel_id=1, replica_groups=mesh['zz'=4,'core'=2,'ctx'=4] {'core','ctx'}, dimensions={0} | all-to-all | bytes 4194304 | tf_op jit(solution)/shard_map/all_to_all | solution.py:387
  1144.9 32.9 %shard_map.286 = bf16[2,4096,384]{2,1,0:T(8,128)(2,1)} custom-call(s32[2,8]{1,0:T(2,128)S(1)} %bitcast.333, s32[2]{0:T(128)S(1)} %copy-done.17, bf16[2,4096,384]{2,1,0:T(8,128)(2,1)} %bitcast.349, bf16[2,4096,128]{2,1,0:T(8,128)(2,1)S(1)} %get-tuple-element.27.o_ref, bf16[2,4096,128]{2,1,0:T(8,128)(2,1)S(1)} %bitcast.328, f32[2,8,4096]{2,1,0:T(8,128)S(1)} %copy-done.19), custom_call_target="tpu_custom_call" | custom-call | flops 42949672960 | bytes 19660800 | tf_op jit(solution)/shard_map/pallas_call | solution.py:165
  1192.8 69.7 %all-to-all-done.7 = bf16[8,1024,384]{1,2,0:T(8,128)(2,1)} async-done(((bf16[8,1024,384]{1,2,0:T(8,128)(2,1)}), bf16[8,1024,384]{1,2,0:T(8,128)(2,1)}, u32[]{:S(2)}, u32[]{:S(2)}) %all-to-all-start.7) | async-done | bytes 6291488 | tf_op jit(solution)/shard_map/all_to_all | solution.py:387
  1314.8 101.7 %reduce-scatter.35.cloned.1.call-done = bf16[544,1088]{1,0:T(8,128)(2,1)} async-done(((bf16[4352,1088]{1,0:T(8,128)(2,1)}), bf16[544,1088]{1,0:T(8,128)(2,1)}) %reduce-scatter.35.cloned.1.call-update) | async-done | bytes 1183760 | tf_op jit(solution)/shard_map/reduce_scatter | solution.py:419
  1421.1 96.0 %reduce-scatter.27.cloned.1.call-done = bf16[136,4352]{1,0:T(8,128)(2,1)} async-done(((bf16[1088,4352]{1,0:T(8,128)(2,1)}), bf16[136,4352]{1,0:T(8,128)(2,1)}) %reduce-scatter.27.cloned.1.call-update) | async-done | bytes 1183760 | tf_op jit(solution)/shard_map/reduce_scatter | solution.py:419
  1522.4 74.3 %reduce-scatter.25.cloned.1.call-done = bf16[136,3264]{1,0:T(8,128)(2,1)} async-done(((bf16[1088,3264]{1,0:T(8,128)(2,1)}), bf16[136,3264]{1,0:T(8,128)(2,1)}) %reduce-scatter.25.cloned.1.call-update) | async-done | bytes 887824 | tf_op jit(solution)/shard_map/reduce_scatter | solution.py:419
  1602.7 33.8 %reduce-scatter.37.cloned.1.call-done = bf16[136,1088]{1,0:T(8,128)(2,1)} async-done(((bf16[1088,1088]{1,0:T(8,128)(2,1)}), bf16[136,1088]{1,0:T(8,128)(2,1)}) %reduce-scatter.37.cloned.1.call-update) | async-done | bytes 295952
  1636.5 106.1 %reduce-scatter.29.cloned.1.call-done = bf16[544,1088]{1,0:T(8,128)(2,1)} async-done(((bf16[4352,1088]{1,0:T(8,128)(2,1)}), bf16[544,1088]{1,0:T(8,128)(2,1)}) %reduce-scatter.29.cloned.1.call-update) | async-done | bytes 1183760 | tf_op jit(solution)/shard_map/reduce_scatter | solution.py:419
  1794.3 52.1 %reduce-scatter.39.cloned.1.call-done = bf16[408,1088]{1,0:T(8,128)(2,1)} async-done(((bf16[1632,1088]{1,0:T(8,128)(2,1)}), bf16[408,1088]{1,0:T(8,128)(2,1)}) %reduce-scatter.39.cloned.1.call-update) | async-done | bytes 887824
  1870.9 30.1 %all-reduce.8.cloned.1.call-done = f32[8,2,1632]{2,1,0:T(2,128)} async-done(((f32[8,2,1632]{2,1,0:T(2,128)}), f32[8,2,1632]{2,1,0:T(2,128)}) %all-reduce.8.cloned.1.call-update) | async-done | bytes 104464
  1920.1 33.4 %all-gather.30.cloned.1.call-done = bf16[1632,1088]{1,0:T(8,128)(2,1)} async-done(((bf16[408,1088]{1,0:T(8,128)(2,1)}), bf16[1632,1088]{1,0:T(8,128)(2,1)}) %all-gather.30.cloned.1.call-update) | async-done | bytes 3551248 | tf_op jit(solution)/shard_map/all_gather | solution.py:423
  (573 shorter events, 744.1 us)
Async XLA Ops:
  20.7 230.9 %all-gather.22.cloned.1.call-start = ((), (), s32[]{:S(2)}) async-start(), calls=%async_computation.21 | async-start | bytes 1310720 | tf_op jit(solution)/shard_map/all_gather | solution.py:400
  100.2 156.2 %all-gather.32.cloned.1.call-start = ((), (), s32[]{:S(2)}) async-start(), calls=%async_computation.34 | async-start | bytes 2820096 | tf_op jit(solution)/shard_map/all_gather | solution.py:375
  101.2 182.0 %all-gather.34.cloned.1.call-start = ((), (), s32[]{:S(2)}) async-start(), calls=%async_computation.35 | async-start | bytes 10653696 | tf_op jit(solution)/shard_map/all_gather | solution.py:375
  105.4 242.9 %all-gather.36.cloned.1.call-start = ((), (), s32[]{:S(2)}) async-start(), calls=%async_computation.36 | async-start | bytes 11280384 | tf_op jit(solution)/shard_map/all_gather | solution.py:375
  110.0 311.5 %all-gather.24.cloned.1.call-start = ((), (), s32[]{:S(2)}) async-start(), calls=%async_computation.22 | async-start | bytes 8146944 | tf_op jit(solution)/shard_map/all_gather | solution.py:375
  247.7 315.8 %all-gather.38.cloned.1.call-start = ((), (), s32[]{:S(2)}) async-start(), calls=%async_computation.37 | async-start | bytes 2820096 | tf_op jit(solution)/shard_map/all_gather | solution.py:375
  248.5 319.3 %all-gather.26.cloned.1.call-start = ((), (), s32[]{:S(2)}) async-start(), calls=%async_computation.23 | async-start | bytes 1310720 | tf_op jit(solution)/shard_map/all_gather | solution.py:400
  425.7 173.4 %all-gather.40.cloned.1.call-start = ((), (), s32[]{:S(2)}) async-start(), calls=%async_computation.38 | async-start | bytes 10653696 | tf_op jit(solution)/shard_map/all_gather | solution.py:375
  426.4 262.0 %all-gather.42.cloned.1.call-start = ((), (), s32[]{:S(2)}) async-start(), calls=%async_computation.39 | async-start | bytes 11280384 | tf_op jit(solution)/shard_map/all_gather | solution.py:375
  820.8 121.0 %all-to-all-start.5 = ((bf16[8,1024,384]{1,2,0:T(8,128)(2,1)}), bf16[8,1024,384]{1,2,0:T(8,128)(2,1)}, u32[]{:S(2)}, u32[]{:S(2)}) async-start(bf16[8,1024,384]{1,2,0:T(8,128)(2,1)} %copy.230), calls=%async_computation.5 | async-start | bytes 12582912 | tf_op jit(solution)/shard_map/all_to_all | solution.py:387
  834.6 357.1 %reduce-scatter.23.cloned.1.call-start = ((), (), s32[]{:S(2)}) async-start(), calls=%async_computation.25 | async-start | bytes 1310720 | tf_op jit(solution)/shard_map/reduce_scatter | solution.py:448
  1033.2 270.2 %reduce-scatter.33.cloned.1.call-start = ((), (), s32[]{:S(2)}) async-start(), calls=%async_computation.31 | async-start | bytes 10653696 | tf_op jit(solution)/shard_map/reduce_scatter | solution.py:419
  1050.5 258.3 %reduce-scatter.31.cloned.1.call-start = ((), (), s32[]{:S(2)}) async-start(), calls=%async_computation.30 | async-start | bytes 8146944 | tf_op jit(solution)/shard_map/reduce_scatter | solution.py:419
  1065.9 248.9 %reduce-scatter.41.cloned.1.call-start = ((), (), s32[]{:S(2)}) async-start(), calls=%async_computation.43 | async-start | bytes 2820096
  1073.6 342.8 %reduce-scatter.35.cloned.1.call-start = ((), (), s32[]{:S(2)}) async-start(), calls=%async_computation.32 | async-start | bytes 11280384 | tf_op jit(solution)/shard_map/reduce_scatter | solution.py:419
  1091.5 425.6 %reduce-scatter.27.cloned.1.call-start = ((), (), s32[]{:S(2)}) async-start(), calls=%async_computation.27 | async-start | bytes 10653696 | tf_op jit(solution)/shard_map/reduce_scatter | solution.py:419
  1191.4 405.3 %reduce-scatter.25.cloned.1.call-start = ((), (), s32[]{:S(2)}) async-start(), calls=%async_computation.26 | async-start | bytes 8146944 | tf_op jit(solution)/shard_map/reduce_scatter | solution.py:419
  1277.4 359.1 %reduce-scatter.37.cloned.1.call-start = ((), (), s32[]{:S(2)}) async-start(), calls=%async_computation.41 | async-start | bytes 2820096
  1285.2 457.5 %reduce-scatter.29.cloned.1.call-start = ((), (), s32[]{:S(2)}) async-start(), calls=%async_computation.28 | async-start | bytes 11280384 | tf_op jit(solution)/shard_map/reduce_scatter | solution.py:419
  1303.4 490.2 %reduce-scatter.43.cloned.1.call-start = ((), (), s32[]{:S(2)}) async-start(), calls=%async_computation.44 | async-start | bytes 4700160
  1421.0 425.4 %reduce-scatter.39.cloned.1.call-start = ((), (), s32[]{:S(2)}) async-start(), calls=%async_computation.42 | async-start | bytes 4700160
  1747.3 153.7 %all-reduce.8.cloned.1.call-start = ((), (), s32[]{:S(2)}) async-start(), calls=%async_computation.40 | async-start | bytes 212992
  1775.3 178.2 %all-gather.30.cloned.1.call-start = ((), (), s32[]{:S(2)}) async-start(), calls=%async_computation.33 | async-start | bytes 4700160 | tf_op jit(solution)/shard_map/all_gather | solution.py:423
  1793.6 211.1 %all-gather.28.cloned.1.call-start = ((), (), s32[]{:S(2)}) async-start(), calls=%async_computation.29 | async-start | bytes 4700160 | tf_op jit(solution)/shard_map/all_gather | solution.py:423
  (129 other events, 4724.6 us)
Sparse Core Ops, SparseCore 0:
  20.8 75.3 all-gather.19
  127.1 32.8 all-gather.31
  162.1 90.0 all-gather.33
  254.3 94.0 all-gather.35
  350.4 70.9 all-gather.23
  423.1 31.5 all-gather.37
  456.5 42.7 all-gather.25
  501.0 91.2 all-gather.39
  594.3 94.0 all-gather.41
  834.7 105.9 reduce-scatter.20
  1033.3 55.1 reduce-scatter.22
  1090.8 100.0 reduce-scatter.32
  1193.1 77.3 reduce-scatter.30
  1273.4 36.7 reduce-scatter.40
  1312.4 104.0 reduce-scatter.34
  1418.6 98.4 reduce-scatter.26
  1519.3 77.3 reduce-scatter.24
  1599.7 36.7 reduce-scatter.36
  1638.7 103.9 reduce-scatter.28
  1745.7 47.7 reduce-scatter.42
  1796.9 49.4 reduce-scatter.38
  1849.3 51.6 all-reduce.7
  1902.8 50.6 all-gather.29
  1955.5 49.0 all-gather.27
  (1 shorter events, 25.1 us)

commit v2 on v1

--- a/solution.py
+++ b/solution.py
@@ -218,10 +218,11 @@
 def one_fwd(q,x,own,B):
     N=x.shape[0]; R=q.shape[0]; NB=N//B
     full=lambda *_:(0,0)
+    last=lambda *_:(0,3)
     return pl.pallas_call(functools.partial(one_fwd_kernel,B=B,NB=NB),
       out_shape=(jax.ShapeDtypeStruct((R,64),bf16),jax.ShapeDtypeStruct((8,R),f32)),
       grid_spec=pltpu.PrefetchScalarGridSpec(num_scalar_prefetch=1,grid=(1,),
-        in_specs=[pl.BlockSpec((R,64),full),pl.BlockSpec((N,128),full)],
+        in_specs=[pl.BlockSpec((R,64),full),pl.BlockSpec((N,128),last)],
         out_specs=[pl.BlockSpec((R,64),full),pl.BlockSpec((8,R),full)],
         scratch_shapes=[pltpu.VMEM((80,N),bf16),pltpu.VMEM((B,B),f32),pltpu.VMEM((80,B),f32)]),
       compiler_params=pltpu.CompilerParams(vmem_limit_bytes=48<<20),
@@ -277,10 +278,11 @@
 def one_bwd(q,x,o,do,lse,own,B):
     N=x.shape[0]; R=q.shape[0]; NB=N//B
     full=lambda *_:(0,0)
+    last=lambda *_:(0,3)
     return pl.pallas_call(functools.partial(one_bwd_kernel,B=B,NB=NB),
       out_shape=(jax.ShapeDtypeStruct((R,64),bf16),jax.ShapeDtypeStruct((N,128),bf16)),
       grid_spec=pltpu.PrefetchScalarGridSpec(num_scalar_prefetch=1,grid=(1,),
-        in_specs=[pl.BlockSpec((R,64),full),pl.BlockSpec((N,128),full),pl.BlockSpec((R,64),full),pl.BlockSpec((R,64),full),pl.BlockSpec((8,R),full)],
+        in_specs=[pl.BlockSpec((R,64),full),pl.BlockSpec((N,128),last),pl.BlockSpec((R,64),full),pl.BlockSpec((R,64),full),pl.BlockSpec((8,R),full)],
         out_specs=[pl.BlockSpec((R,64),full),pl.BlockSpec((N,128),full)],
         scratch_shapes=[pltpu.VMEM((N,128),f32),pltpu.VMEM((64,B),f32)]),
       compiler_params=pltpu.CompilerParams(vmem_limit_bytes=48<<20),
@@ -327,7 +329,6 @@
     slots, rows, width = tokens.shape
     C = lax.axis_size("ctx")
     me = lax.axis_index("ctx")
-    group = ("core", "ctx") if S == 2 else ("ctx",)
     N = rows * C
     B = rows // 2
     NB = 2 * C
@@ -341,8 +342,13 @@
     inverse = jnp.sum(jnp.where(order[None, :] == steps[:, None], steps[None, :], 0), axis=1).astype(jnp.int32)
     count = (lengths + (B - 1)) // B
     meta = jnp.concatenate([inverse, count])
-    both = lax.all_gather(meta, "core") if S == 2 else meta[None]
-    inv, nb = both[:, :NB], both[:, NB]
+    def swap(x):
+        return lax.ppermute(x, "core", [(0, 1), (1, 0)])
+
+    metas = [meta, swap(meta)][:S]
+    phase_inv = [t[None, :NB] for t in metas]
+    phase_nb = [t[NB:] for t in metas]
+    core = lax.axis_index("core")
     own = jnp.concatenate([inverse, lax.dynamic_slice_in_dim(order, 2 * me, 2, 0), count])
     own_pos = (lax.dynamic_slice_in_dim(order, 2 * me, 2, 0)[:, None] * B + jnp.arange(B, dtype=jnp.int32)).reshape(rows, 1)
     live = (own_pos < lengths[0]).astype(f32)
@@ -383,8 +389,17 @@
             fetch(down_weight[layer]),
         ))
 
+    def ordered(x, axis):
+        if S == 1:
+            return x
+        a, b = jnp.split(x, 2, axis=axis)
+        return jnp.where(core == 0, jnp.concatenate([a, b], axis), jnp.concatenate([b, a], axis))
+
     def exchange(x):
-        return lax.all_to_all(x, group, 0, 0)
+        return lax.all_to_all(x, "ctx", 0, 0)
+
+    def after(x, *others):
+        return lax.optimization_barrier((x,) + others)
 
     stream = x_tokens.astype(f32)
     records = []
@@ -394,16 +409,37 @@
         n1 = (xhat * vector(0, layer) + vector(1, layer)).astype(bf16)
         q_b, v_b = vector(2, layer), vector(3, layer)
         bias = pack(jnp.concatenate([q_b, jnp.zeros_like(q_b), v_b])[None])[0]
-        wide = jnp.einsum("rd,dgc->grc", n1, qkv_w[:, :G * 384].reshape(width, G, 384), preferred_element_type=f32)
-        wide = (wide + bias[:G * 384].reshape(G, 1, 384)).astype(bf16)
+        wide = []
+        for s in range(S):
+            half = C * 384
+            first = half * (core if s == 0 else 1 - core) if S == 2 else 0
+            w = lax.dynamic_slice_in_dim(qkv_w, first, half, 1).reshape(width, C, 384)
+            b = lax.dynamic_slice_in_dim(bias, first, half, 0).reshape(C, 1, 384)
+            wide.append((jnp.einsum("rd,dgc->grc", n1, w, preferred_element_type=f32) + b).astype(bf16))
+        if S == 2:
+            wide[1] = swap(wide[1])
         tail = (jnp.dot(n1, qkv_w[:, G * 384:], preferred_element_type=f32) + bias[G * 384:]).astype(bf16)
-        kv16 = lax.all_gather(tail[:, :128], "ctx", axis=0, tiled=True)
+        kv16 = jnp.broadcast_to(tail[None, :, :128], (C, rows, 128))
         q16 = tail[:, 128:]
-        heads = exchange(wide).reshape(S, N, 384)
-        o, lse = flash_fwd(heads, inv, nb, B)
-        o16, lse16 = one_fwd(q16, kv16, own, B)
-        o_back = exchange(o.reshape(G, rows, 128))
-        mixed = jnp.concatenate([jnp.transpose(o_back, (1, 0, 2)).reshape(rows, HW), o16], axis=1)
+        heads, o, lse, o_back = [], [], [], []
+        for s in range(S):
+            t = wide[s]
+            if s == S - 1:
+                t = jnp.concatenate([t, kv16], axis=2)
+            if s:
+                t, heads[0] = after(t, heads[0])
+            heads.append(exchange(t).reshape(1, N, -1))
+        for s in range(S):
+            o_s, lse_s = flash_fwd(heads[s], phase_inv[s], phase_nb[s], B)
+            o.append(o_s)
+            lse.append(lse_s)
+            t = o_s.reshape(C, rows, 128)
+            if s:
+                t, o_back[0] = after(t, o_back[0])
+            o_back.append(exchange(swap(t) if s else t))
+        o16, lse16 = one_fwd(q16, heads[-1][0], own, B)
+        o_all = ordered(jnp.concatenate(o_back, axis=0), 0)
+        mixed = jnp.concatenate([jnp.transpose(o_all, (1, 0, 2)).reshape(rows, HW), o16], axis=1)
         m = stream + jnp.dot(mixed, out_w, preferred_element_type=f32) + vector(4, layer)
         xhat2, _ = norm_parts(m)
         n2 = (xhat2 * vector(5, layer) + vector(6, layer)).astype(bf16)
@@ -411,7 +447,7 @@
         a, slope = gelu_parts(u)
         a = a.astype(bf16)
         slope = slope.astype(bf16)
-        records.append((stream, n1, heads, kv16, q16, o, lse, o16, lse16, mixed, m, n2, a, slope))
+        records.append((stream, n1, heads, q16, o, lse, o16, lse16, mixed, m, n2, a, slope))
         stream = m + jnp.dot(a, down_w, preferred_element_type=f32) + vector(7, layer)
     activations = (stream * live).astype(bf16)[None]
 
@@ -419,44 +455,82 @@
         return lax.psum_scatter(g.astype(bf16), FS, scatter_dimension=0, tiled=True)
 
     def reduce_ctx(g):
-        t = lax.psum_scatter(g, "ctx", scatter_dimension=0, tiled=True)
-        return lax.all_gather(t, "ctx", axis=0, tiled=True).astype(f32)
+        return lax.psum(g, "ctx").astype(f32)
 
     grad = cotangent[0].astype(f32) * live
     matrices = [None] * L
+    fours = [None] * L
     small = [None] * L
+
+    def finish(layer):
+        d_four, d_up, d_down = fours[layer]
+        parts = [jnp.transpose(t.reshape(shard, 4, width), (1, 0, 2)).reshape(4 * shard, width) for t in (d_four, d_up)]
+        matrices[layer] = reduce_ctx(jnp.concatenate(parts + [d_down], axis=0))
+
     for layer in reversed(range(L)):
-        stream_in, n1, heads, kv16, q16, o, lse, o16, lse16, mixed, m, n2, a, slope = records[layer]
+        stream_in, n1, heads, q16, o, lse, o16, lse16, mixed, m, n2, a, slope = records[layer]
         qkv_w, out_w, up_w, down_w = weights[layer]
         gb = grad.astype(bf16)
         d_down_b = jnp.sum(gb.astype(f32), axis=0)
-        d_down = reduce_fsdp(jnp.einsum("rf,rd->fd", a, gb, preferred_element_type=f32))
+        d_down = jnp.einsum("rf,rd->fd", a, gb, preferred_element_type=f32).astype(bf16)
+        gb, d_down = after(gb, d_down)
+        d_down = reduce_fsdp(d_down)
         du = (jnp.einsum("rd,fd->rf", gb, down_w, preferred_element_type=f32) * slope.astype(f32)).astype(bf16)
         d_up_b = jnp.sum(du.astype(f32), axis=0)
-        d_up = reduce_fsdp(jnp.einsum("rd,rf->df", n2, du, preferred_element_type=f32))
+        d_up = jnp.einsum("rd,rf->df", n2, du, preferred_element_type=f32).astype(bf16)
+        du, d_up = after(du, d_up)
+        d_up = reduce_fsdp(d_up)
         dn2 = jnp.einsum("rf,df->rd", du, up_w, preferred_element_type=f32)
         back, d_gain2, d_bias2 = norm_back(dn2, m, vector(5, layer))
         gm = grad + back
         gmb = gm.astype(bf16)
         d_out_b = jnp.sum(gmb.astype(f32), axis=0)
-        d_out = reduce_fsdp(jnp.einsum("rd,re->de", mixed, gmb, preferred_element_type=f32))
-        d_o = jnp.einsum("re,gce->grc", gmb, out_w[:HW].reshape(G, 128, width), preferred_element_type=f32).astype(bf16)
+        d_out = jnp.einsum("rd,re->de", mixed, gmb, preferred_element_type=f32).astype(bf16)
+        d_o = []
+        for s in range(S):
+            first = C * 128 * (core if s == 0 else 1 - core) if S == 2 else 0
+            w = lax.dynamic_slice_in_dim(out_w, first, C * 128, 0).reshape(C, 128, width)
+            d_o.append(jnp.einsum("re,gce->grc", gmb, w, preferred_element_type=f32).astype(bf16))
         d_o16 = jnp.einsum("re,ce->rc", gmb, out_w[HW:], preferred_element_type=f32).astype(bf16)
-        d_oh = exchange(d_o).reshape(S, N, 128)
-        d_heads = flash_bwd(heads, o, d_oh, lse, inv, nb, B)
-        dq16, dkv16 = one_bwd(q16, kv16, o16, d_o16, lse16, own, B)
-        dkv16 = lax.psum_scatter(dkv16, "ctx", scatter_dimension=0, tiled=True)
-        d_wide = exchange(d_heads.reshape(G, rows, 384))
+        dq16, dkv16 = one_bwd(q16, heads[-1][0], o16, d_o16, lse16, own, B)
+        d_oh, d_wide = [], []
+        for s in range(S):
+            t = d_o[s]
+            if s:
+                t = swap(t)
+            if s == S - 1:
+                t = jnp.concatenate([t, dkv16.reshape(C, rows, 128)], axis=2)
+            if s == S - 1 and layer < L - 1:
+                t, fours[layer + 1] = after(t, fours[layer + 1])
+                finish(layer + 1)
+            if s:
+                t, d_oh[0] = after(t, d_oh[0])
+            d_oh.append(exchange(t).reshape(1, N, -1))
+        dkv16 = jnp.sum(d_oh[-1].reshape(C, rows, 256)[:, :, 128:].astype(f32), axis=0)
+        for s in range(S):
+            t = flash_bwd(heads[s], o[s], d_oh[s], lse[s], phase_inv[s], phase_nb[s], B)
+            t = t.reshape(C, rows, 384)
+            if s:
+                t, d_wide[0], d_down = after(t, d_wide[0], d_down)
+            d_wide.append(exchange(swap(t) if s else t))
+        d_wide = ordered(jnp.concatenate(d_wide, axis=0), 0)
         d_tail = jnp.concatenate([dkv16.astype(bf16), dq16], axis=1)
         d_row = jnp.concatenate([jnp.transpose(d_wide, (1, 0, 2)).reshape(rows, G * 384), d_tail], axis=1)
-        d_qkv = reduce_fsdp(jnp.einsum("rd,rc->dc", n1, d_row, preferred_element_type=f32))
+        d_qkv = jnp.einsum("rd,rc->dc", n1, d_row, preferred_element_type=f32).astype(bf16)
+        d_four = jnp.concatenate([d_qkv, d_out], axis=1)
+        if layer:
+            d_row, d_four = after(d_row, d_four)
+            d_row, d_up = after(d_row, d_up)
+        else:
+            d_four, matrices[layer + 1] = after(d_four, matrices[layer + 1])
+        d_four = reduce_fsdp(d_four)
         sums = unpack(jnp.sum(d_row.astype(f32), axis=0)[None])[0]
         dn1 = jnp.einsum("rc,dc->rd", d_row, qkv_w, preferred_element_type=f32)
         back, d_gain1, d_bias1 = norm_back(dn1, stream_in, vector(0, layer))
         grad = gm + back
-        parts = [jnp.transpose(d_qkv.reshape(shard, 3, width), (1, 0, 2)).reshape(3 * shard, width), d_out,
-                 jnp.transpose(d_up.reshape(shard, 4, width), (1, 0, 2)).reshape(4 * shard, width), d_down]
-        matrices[layer] = reduce_ctx(jnp.concatenate(parts, axis=0))
+        fours[layer] = (d_four, d_up, d_down)
+        if layer == 0:
+            finish(0)
         small[layer] = jnp.concatenate([
             t.reshape(-1, n) for t, n in (
                 (d_gain1, shard), (d_bias1, shard), (sums[:width], shard), (sums[2 * width:], shard), (d_out_b, shard),

time: 2070 us -> 1860 us (0.90)
  waiting for transfers between devices: 1030 us -> 452 us
  Pallas kernels: 125 us -> 386 us
  blocking collectives: 177 us -> 48 us
  local copies, waits for them, and re-layouts: 195 us -> 295 us
  other arithmetic: 83.8 us -> 166 us
  starting transfers between devices: 25 us -> 98.6 us
    reduce_scatter x6 -> x4, waiting for transfers between devices: 378 us -> 73.8 us  [reduce_fsdp(): return lax.psum_scatter(g.astype(bf16), FS, scatter_dimension=0, tiled=True)]
    pallas_call x2 -> x4, Pallas kernels: 65.7 us -> 205 us  [flash_bwd(): pl.pallas_call(functools.partial(bwd_kernel, B=B, NB=NB), out_shape=jax.S...]
    psum x0 -> x2, waiting for transfers between devices: none -> 133 us  [reduce_ctx(): return lax.psum(g, 'ctx').astype(f32)]
    all_to_all x3 -> x1, blocking collectives: 143 us -> 15.3 us  [exchange(): return lax.all_to_all(x, 'ctx', 0, 0)]
    unnamed x30 -> x20, waiting for transfers between devices: 136 us -> 15.5 us
    reduce_scatter x2 -> x0, waiting for transfers between devices: 106 us -> none  [local(): dkv16 = lax.psum_scatter(dkv16, 'ctx', scatter_dimension=0, tiled=True)]
    pallas_call x2 -> x4, Pallas kernels: 42.7 us -> 133 us  [flash_fwd(): pl.pallas_call(functools.partial(fwd_kernel, B=B, NB=NB), out_shape=(jax....]
    all_to_all x5 -> x15, waiting for transfers between devices: 169 us -> 96.9 us  [exchange(): return lax.all_to_all(x, 'ctx', 0, 0)]
  transfers between devices with their start and end apart: 30 -> 41, of which waited for: 19 -> 16; matrix products, arithmetic and copies ran while one was open for 21% -> 41% of each run, Pallas kernels for 4% -> 21%
where the time goes in v2:
time: 1860 us
  waiting for transfers between devices  452 us (24%)
  matrix products  399 us (21%)
  Pallas kernels  386 us (21%)
  local copies, waits for them, and re-layouts  295 us (16%)
  other arithmetic  166 us (9%)
  starting transfers between devices  98.6 us (5%)
  blocking collectives  48 us (3%)
    pallas_call x4, Pallas kernels, flash_bwd(): pl.pallas_call(functools.partial(bwd_kernel, B=B, NB=NB), out_shape=jax.S...  205 us
    psum x2, waiting for transfers between devices, reduce_ctx(): return lax.psum(g, 'ctx').astype(f32)  133 us
    pallas_call x4, Pallas kernels, flash_fwd(): pl.pallas_call(functools.partial(fwd_kernel, B=B, NB=NB), out_shape=(jax....  133 us
    all_gather x8, waiting for transfers between devices, fetch(): return lax.all_gather(w.astype(bf16), FS, axis=0, tiled=True)  116 us
    all_to_all x15, waiting for transfers between devices, exchange(): return lax.all_to_all(x, 'ctx', 0, 0)  96.9 us
    reduce_scatter x4, waiting for transfers between devices, reduce_fsdp(): return lax.psum_scatter(g.astype(bf16), FS, scatter_dimension=0, tiled=True)  73.8 us
    dot_general x2, matrix products, local(): u = jnp.dot(n2, up_w, preferred_element_type=f32) + vector(8, layer)  70.1 us
    all_to_all x15, starting transfers between devices, exchange(): return lax.all_to_all(x, 'ctx', 0, 0)  66.8 us
  transfers between devices with their start and end apart: 41, of which 16 were waited for; matrix products, arithmetic and copies ran while one was open for 41% of the time, Pallas kernels for 21%

profile of v2, /device:TPU:0, one launch (start us, length us, event | category | flops | bytes accessed | tf_op | source)
XLA Modules:
  0.0 1863.1 jit_solution(10291492340502519277)
XLA Ops:
  51.7 42.5 %all-gather.15.cloned.1.call-done = bf16[1088,3264]{1,0:T(8,128)(2,1)} async-done(((bf16[136,3264]{1,0:T(8,128)(2,1)}), bf16[1088,3264]{1,0:T(8,128)(2,1)}) %all-gather.15.cloned.1.call-update) | async-done | bytes 7102480 | tf_op jit(solution)/shard_map/all_gather | solution.py:381
  94.2 73.5 %all-gather.17.cloned.1.call-done = bf16[1088,3264]{1,0:T(8,128)(2,1)} async-done(((bf16[136,3264]{1,0:T(8,128)(2,1)}), bf16[1088,3264]{1,0:T(8,128)(2,1)}) %all-gather.17.cloned.1.call-update) | async-done | bytes 7102480 | tf_op jit(solution)/shard_map/all_gather | solution.py:381
  217.2 32.8 %all-to-all-done = bf16[4,1024,384]{1,2,0:T(8,128)(2,1)} async-done(((bf16[4,1024,384]{1,2,0:T(8,128)(2,1)}), bf16[4,1024,384]{1,2,0:T(8,128)(2,1)}, u32[]{:S(2)}, u32[]{:S(2)}) %all-to-all-start) | async-done | bytes 3145760 | tf_op jit(solution)/shard_map/all_to_all | solution.py:399
  266.7 40.8 %shard_map.281 = (bf16[1,4096,128]{2,1,0:T(8,128)(2,1)S(1)}, f32[1,8,4096]{2,1,0:T(8,128)S(1)}) custom-call(s32[1,8]{1,0:T(1,128)S(1)} %bitcast.393, s32[1]{0:T(128)S(6)} %select_n.66.nb_ref, bf16[1,4096,384]{2,1,0:T(8,128)(2,1)S(1)} %bitcast.377), custom_call_target="tpu_custom_call" | custom-call | flops 8589934592 | bytes 4194304 | tf_op jit(solution)/shard_map/pallas_call | solution.py:87
  324.0 25.4 %shard_map.280 = (bf16[1,4096,128]{2,1,0:T(8,128)(2,1)S(1)}, f32[1,8,4096]{2,1,0:T(8,128)S(1)}) custom-call(s32[1,8]{1,0:T(1,128)S(1)} %slice_bitcast_fusion.20.inv_ref, s32[1]{0:T(128)} %slice.302.nb_ref, bf16[1,4096,512]{2,1,0:T(8,128)(2,1)S(1)} %bitcast.371), custom_call_target="tpu_custom_call" | custom-call | flops 8589934592 | bytes 4194304 | tf_op jit(solution)/shard_map/pallas_call | solution.py:87
  409.0 35.1 %multiply_convert_fusion.3 = (bf16[1024,4352]{1,0:T(8,128)(2,1)}, f32[1024,4352]{1,0:T(8,128)}) fusion(f32[4352]{0:T(1024)S(1)} %add.360, bf16[1,1088,4352]{2,1,0:T(8,128)(2,1)} %all-gather.21.cloned.1.call-done, f32[1024,1088]{0,1:T(8,128)} %copy-done.47, f32[1088]{0:T(1024)S(1)} %add.357, f32[1088]{0:T(1024)S(1)} %mul.364, f32[1024]{0:T(1024)S(1)} %add_rsqrt_fusion.2, ...), kind=kOutput, calls=%fused_computation.17 | convolution fusion | flops 9809756160 | bytes 40699392 | tf_op jit(solution)/shard_map/dot_general | solution.py:446
  444.1 17.8 fusion.130
  486.7 33.4 %all-to-all-done.4 = bf16[4,1024,384]{1,2,0:T(8,128)(2,1)} async-done(((bf16[4,1024,384]{1,2,0:T(8,128)(2,1)}), bf16[4,1024,384]{1,2,0:T(8,128)(2,1)}, u32[]{:S(2)}, u32[]{:S(2)}) %all-to-all-start.4) | async-done | bytes 3145760 | tf_op jit(solution)/shard_map/all_to_all | solution.py:399
  534.2 41.2 %shard_map.284 = (bf16[1,4096,128]{2,1,0:T(8,128)(2,1)S(1)}, f32[1,8,4096]{2,1,0:T(8,128)S(1)}) custom-call(s32[1,8]{1,0:T(1,128)S(1)} %bitcast.394, s32[1]{0:T(128)S(6)} %select_n.66.nb_ref, bf16[1,4096,384]{2,1,0:T(8,128)(2,1)S(1)} %bitcast.379), custom_call_target="tpu_custom_call" | custom-call | flops 8589934592 | bytes 4194304 | tf_op jit(solution)/shard_map/pallas_call | solution.py:87
  594.1 25.3 %shard_map.283 = (bf16[1,4096,128]{2,1,0:T(8,128)(2,1)S(1)}, f32[1,8,4096]{2,1,0:T(8,128)S(1)}) custom-call(s32[1,8]{1,0:T(1,128)S(1)} %slice_bitcast_fusion.20.inv_ref, s32[1]{0:T(128)} %slice.302.nb_ref, bf16[1,4096,512]{2,1,0:T(8,128)(2,1)S(1)} %bitcast.375), custom_call_target="tpu_custom_call" | custom-call | flops 8589934592 | bytes 4194304 | tf_op jit(solution)/shard_map/pallas_call | solution.py:87
  673.8 35.0 %multiply_convert_fusion.2 = (bf16[1024,4352]{1,0:T(8,128)(2,1)}, f32[1024,4352]{1,0:T(8,128)}) fusion(f32[4352]{0:T(1024)S(1)} %add.393, bf16[1,1088,4352]{2,1,0:T(8,128)(2,1)} %all-gather.27.cloned.1.call-done, f32[1024,1088]{0,1:T(8,128)} %get-tuple-element.263, f32[1088]{0:T(1024)S(1)} %add.390, f32[1088]{0:T(1024)S(1)} %mul.388, ...), kind=kOutput, calls=%fused_computation.16 | convolution fusion | flops 9809756160 | bytes 40699392 | tf_op jit(solution)/shard_map/dot_general | solution.py:446
  743.2 31.6 %convert_reduce_fusion = (f32[4352]{0:T(1024)}, bf16[1024,4352]{1,0:T(8,128)(2,1)S(1)}) fusion(f32[1024,4352]{1,0:T(8,128)} %get-tuple-element.265, f32[4352]{0:T(1024)S(1)} %add.393, bf16[1024,1088]{0,1:T(8,128)(2,1)} %get-tuple-element.81, bf16[1,4352,1088]{2,1,0:T(8,128)(2,1)} %all-gather.29.cloned.1.call-done), kind=kOutput, calls=%fused_computation.10 | convolution fusion | flops 9835376640 | bytes 38471680 | tf_op jit(solution)/shard_map/rd,fd->rf/dot_general | solution.py:478
  793.7 19.4 %multiply_reduce_fusion = (f32[1088]{0:T(1024)}, f32[1024]{0:T(1024)S(1)}, f32[1024]{0:T(1024)S(1)}, f32[1088]{0:T(1024)}, f32[1024,1088]{0,1:T(8,128)S(1)}) fusion(f32[1024,1088]{0,1:T(8,128)} %get-tuple-element.263, f32[1024]{0:T(1024)S(1)} %copy-done.102, f32[1024]{0:T(1024)S(1)} %copy-done.98, f32[1088]{0:T(1024)S(1)} %copy-done.91, ...), kind=kOutput, calls=%fused_computation.86 | convolution fusion | flops 9707253760 | bytes 27325184 | tf_op jit(solution)/shard_map/rf,df->rd/dot_general | solution.py:483
  858.4 62.4 %shard_map.288 = bf16[1,4096,384]{2,1,0:T(8,128)(2,1)S(1)} custom-call(s32[1,8]{1,0:T(1,128)S(1)} %bitcast.395, s32[1]{0:T(128)S(6)} %select_n.66.nb_ref, bf16[1,4096,384]{2,1,0:T(8,128)(2,1)} %bitcast.380, bf16[1,4096,128]{2,1,0:T(8,128)(2,1)S(1)} %copy-done.13, bf16[1,4096,128]{2,1,0:T(8,128)(2,1)S(1)} %bitcast.389, f32[1,8,4096]{2,1,0:T(8,128)S(1)} %copy-done.38), custom_call_target="tpu_custom_call" | custom-call | flops 21474836480 | bytes 9830400 | tf_op jit(solution)/shard_map/pallas_call | solution.py:165
  932.3 40.4 %shard_map.287 = bf16[1,4096,384]{2,1,0:T(8,128)(2,1)} custom-call(s32[1,8]{1,0:T(1,128)S(1)} %copy-done.30, s32[1]{0:T(128)} %slice.302.nb_ref, bf16[1,4096,512]{2,1,0:T(8,128)(2,1)} %bitcast.374, bf16[1,4096,128]{2,1,0:T(8,128)(2,1)S(1)} %copy-done.11, bf16[1,4096,256]{2,1,0:T(8,128)(2,1)S(1)} %bitcast.384, f32[1,8,4096]{2,1,0:T(8,128)S(1)} %copy-done.34), custom_call_target="tpu_custom_call" | custom-call | flops 21474836480 | bytes 9830400 | tf_op jit(solution)/shard_map/pallas_call | solution.py:165
  997.5 27.4 %all-to-all-done.11 = bf16[4,1024,384]{1,2,0:T(8,128)(2,1)S(1)} async-done(((bf16[4,1024,384]{1,2,0:T(8,128)(2,1)}), bf16[4,1024,384]{1,2,0:T(8,128)(2,1)S(1)}, u32[]{:S(2)}, u32[]{:S(2)}) %all-to-all-start.11) | async-done | bytes 3145760 | tf_op jit(solution)/shard_map/all_to_all | solution.py:399
  1121.1 29.7 %convert_reduce_fusion.1 = (f32[4352]{0:T(1024)}, bf16[1024,4352]{1,0:T(8,128)(2,1)}) fusion(f32[1024,4352]{1,0:T(8,128)} %get-tuple-element.259, f32[4352]{0:T(1024)S(1)} %copy-done.125, bf16[1024,1088]{0,1:T(8,128)(2,1)S(1)} %copy-done.68, bf16[1,4352,1088]{2,1,0:T(8,128)(2,1)} %all-gather.23.cloned.1.call-done), kind=kOutput, calls=%fused_computation.11 | convolution fusion | flops 9835376640 | bytes 38471680 | tf_op jit(solution)/shard_map/rd,fd->rf/dot_general | solution.py:478
  1167.2 19.8 %multiply_reduce_fusion.2 = (f32[1088]{0:T(1024)}, f32[1024]{0:T(1024)S(1)}, f32[1024]{0:T(1024)S(1)}, f32[1088]{0:T(1024)}, f32[1024,1088]{0,1:T(8,128)}) fusion(f32[1024,1088]{0,1:T(8,128)} %copy-done.47, f32[1024]{0:T(1024)S(1)} %copy-done.129, f32[1024]{0:T(1024)S(1)} %copy-done.104, f32[1088]{0:T(1024)S(1)} %copy-done.109, ...), kind=kOutput, calls=%fused_computation.90 | convolution fusion | flops 9707253760 | bytes 27325184 | tf_op jit(solution)/shard_map/rf,df->rd/dot_general | solution.py:483
  1263.9 62.4 %shard_map.291 = bf16[1,4096,384]{2,1,0:T(8,128)(2,1)S(1)} custom-call(s32[1,8]{1,0:T(1,128)S(1)} %bitcast.396, s32[1]{0:T(128)S(6)} %select_n.66.nb_ref, bf16[1,4096,384]{2,1,0:T(8,128)(2,1)} %bitcast.378, bf16[1,4096,128]{2,1,0:T(8,128)(2,1)S(1)} %copy-done.9, bf16[1,4096,128]{2,1,0:T(8,128)(2,1)S(1)} %bitcast.390, f32[1,8,4096]{2,1,0:T(8,128)S(1)} %copy-done.36), custom_call_target="tpu_custom_call" | custom-call | flops 21474836480 | bytes 9830400 | tf_op jit(solution)/shard_map/pallas_call | solution.py:165
  1339.8 40.3 %shard_map.290 = bf16[1,4096,384]{2,1,0:T(8,128)(2,1)} custom-call(s32[1,8]{1,0:T(1,128)S(1)} %copy-done.30, s32[1]{0:T(128)} %slice.302.nb_ref, bf16[1,4096,512]{2,1,0:T(8,128)(2,1)} %bitcast.370, bf16[1,4096,128]{2,1,0:T(8,128)(2,1)S(1)} %copy-done.7, bf16[1,4096,256]{2,1,0:T(8,128)(2,1)S(1)} %bitcast.383, f32[1,8,4096]{2,1,0:T(8,128)S(1)} %copy-done.32), custom_call_target="tpu_custom_call" | custom-call | flops 21474836480 | bytes 9830400 | tf_op jit(solution)/shard_map/pallas_call | solution.py:165
  1403.4 49.4 %all-reduce.5.cloned.1.call-done = bf16[1632,1088]{1,0:T(8,128)(2,1)} async-done(((bf16[1632,1088]{1,0:T(8,128)(2,1)}), bf16[1632,1088]{1,0:T(8,128)(2,1)}) %all-reduce.5.cloned.1.call-update) | async-done | bytes 3551248 | tf_op jit(solution)/shard_map/psum | solution.py:458
  1516.7 35.8 %reduce-scatter.17.cloned.1.call-done = bf16[136,4352]{1,0:T(8,128)(2,1)} async-done(((bf16[1088,4352]{1,0:T(8,128)(2,1)}), bf16[136,4352]{1,0:T(8,128)(2,1)}) %reduce-scatter.17.cloned.1.call-update) | async-done | bytes 1183760 | tf_op jit(solution)/shard_map/reduce_scatter | solution.py:455
  1615.1 38.0 %reduce-scatter.15.cloned.1.call-done = bf16[136,4352]{1,0:T(8,128)(2,1)} async-done(((bf16[1088,4352]{1,0:T(8,128)(2,1)}), bf16[136,4352]{1,0:T(8,128)(2,1)}) %reduce-scatter.15.cloned.1.call-update) | async-done | bytes 1183760 | tf_op jit(solution)/shard_map/reduce_scatter | solution.py:455
  1724.6 83.8 %all-reduce.7.cloned.1.call-done = bf16[1632,1088]{1,0:T(8,128)(2,1)} async-done(((bf16[1632,1088]{1,0:T(8,128)(2,1)}), bf16[1632,1088]{1,0:T(8,128)(2,1)}) %all-reduce.7.cloned.1.call-update) | async-done | bytes 3551248 | tf_op jit(solution)/shard_map/psum | solution.py:458
  (727 shorter events, 902.3 us)
Async XLA Ops:
  7.2 87.0 %all-gather.15.cloned.1.call-start = ((), (), s32[]{:S(2)}) async-start(), calls=%async_computation.22 | async-start | bytes 8146944 | tf_op jit(solution)/shard_map/all_gather | solution.py:381
  18.4 149.3 %all-gather.17.cloned.1.call-start = ((), (), s32[]{:S(2)}) async-start(), calls=%async_computation.23 | async-start | bytes 8146944 | tf_op jit(solution)/shard_map/all_gather | solution.py:381
  22.2 378.2 %all-gather.19.cloned.1.call-start = ((), (), s32[]{:S(2)}) async-start(), calls=%async_computation.30 | async-start | bytes 2820096 | tf_op jit(solution)/shard_map/all_gather | solution.py:381
  23.2 385.7 %all-gather.21.cloned.1.call-start = ((), (), s32[]{:S(2)}) async-start(), calls=%async_computation.31 | async-start | bytes 10653696 | tf_op jit(solution)/shard_map/all_gather | solution.py:381
  27.5 416.7 %all-gather.23.cloned.1.call-start = ((), (), s32[]{:S(2)}) async-start(), calls=%async_computation.32 | async-start | bytes 11280384 | tf_op jit(solution)/shard_map/all_gather | solution.py:381
  194.6 58.9 %collective-permute-start.1 = (bf16[4,1024,384]{1,2,0:T(8,128)(2,1)}, bf16[4,1024,384]{1,2,0:T(8,128)(2,1)}, u32[]{:S(2)}, u32[]{:S(2)}) collective-permute-start(bf16[4,1024,384]{1,2,0:T(8,128)(2,1)} %fusion.62), channel_id=1, source_target_pairs={{0,4},{4,0},{1,5},{5,1},{2,6},{6,2},{3,7},{7,3},{8,12},{12,8},{9,1... | collective-permute-start | bytes 9437192 | tf_op jit(solution)/shard_map/ppermute | solution.py:346
  213.3 448.6 %all-gather.25.cloned.1.call-start = ((), (), s32[]{:S(2)}) async-start(), calls=%async_computation.33 | async-start | bytes 2820096 | tf_op jit(solution)/shard_map/all_gather | solution.py:381
  259.0 52.4 %all-to-all-start.1 = ((bf16[4,1024,512]{1,2,0:T(8,128)(2,1)}), bf16[4,1024,512]{1,2,0:T(8,128)(2,1)}, u32[]{:S(2)}, u32[]{:S(2)}) async-start(bf16[4,1024,512]{1,2,0:T(8,128)(2,1)} %pad_maximum_fusion.6), calls=%async_computation.1 | async-start | bytes 8388608 | tf_op jit(solution)/shard_map/all_to_all | solution.py:399
  264.1 409.7 %all-gather.27.cloned.1.call-start = ((), (), s32[]{:S(2)}) async-start(), calls=%async_computation.34 | async-start | bytes 10653696 | tf_op jit(solution)/shard_map/all_gather | solution.py:381
  483.0 260.2 %all-gather.29.cloned.1.call-start = ((), (), s32[]{:S(2)}) async-start(), calls=%async_computation.35 | async-start | bytes 11280384 | tf_op jit(solution)/shard_map/all_gather | solution.py:381
  529.4 52.8 %all-to-all-start.5 = ((bf16[4,1024,512]{1,2,0:T(8,128)(2,1)}), bf16[4,1024,512]{1,2,0:T(8,128)(2,1)}, u32[]{:S(2)}, u32[]{:S(2)}) async-start(bf16[4,1024,512]{1,2,0:T(8,128)(2,1)} %pad_maximum_fusion.7), calls=%async_computation.5 | async-start | bytes 8388608 | tf_op jit(solution)/shard_map/all_to_all | solution.py:399
  643.4 329.3 %reduce-scatter.19.cloned.1.call-start = ((), (), s32[]{:S(2)}) async-start(), calls=%async_computation.36 | async-start | bytes 11280384
  738.4 324.3 %reduce-scatter.11.cloned.1.call-start = ((), (), s32[]{:S(2)}) async-start(), calls=%async_computation.24 | async-start | bytes 10653696 | tf_op jit(solution)/shard_map/reduce_scatter | solution.py:455
  850.5 73.2 %all-to-all-start.9 = ((bf16[4,1024,256]{1,2,0:T(8,128)(2,1)}), bf16[4,1024,256]{1,2,0:T(8,128)(2,1)}, u32[]{:S(2)}, u32[]{:S(2)}) async-start(bf16[4,1024,256]{1,2,0:T(8,128)(2,1)} %pad_maximum_fusion.13), calls=%async_computation.9 | async-start | bytes 4194304 | tf_op jit(solution)/shard_map/all_to_all | solution.py:399
  923.7 51.6 %all-to-all-start.10 = ((bf16[4,1024,384]{1,2,0:T(8,128)(2,1)}), bf16[4,1024,384]{1,2,0:T(8,128)(2,1)}, u32[]{:S(2)}, u32[]{:S(2)}) async-start(bf16[4,1024,384]{1,2,0:T(8,128)(2,1)} %copy.427), calls=%async_computation.10 | async-start | bytes 6291456 | tf_op jit(solution)/shard_map/all_to_all | solution.py:399
  988.5 227.0 %reduce-scatter.13.cloned.1.call-start = ((), (), s32[]{:S(2)}) async-start(), calls=%async_computation.25 | async-start | bytes 10653696 | tf_op jit(solution)/shard_map/reduce_scatter | solution.py:455
  1062.7 271.6 %reduce-scatter.21.cloned.1.call-start = ((), (), s32[]{:S(2)}) async-start(), calls=%async_computation.37 | async-start | bytes 11280384
  1119.5 333.4 %all-reduce.5.cloned.1.call-start = ((), (), s32[]{:S(2)}) async-start(), calls=%async_computation.26 | async-start | bytes 7520256 | tf_op jit(solution)/shard_map/psum | solution.py:458
  1235.8 316.7 %reduce-scatter.17.cloned.1.call-start = ((), (), s32[]{:S(2)}) async-start(), calls=%async_computation.28 | async-start | bytes 10653696 | tf_op jit(solution)/shard_map/reduce_scatter | solution.py:455
  1256.9 72.3 %all-to-all-start.13 = ((bf16[4,1024,256]{1,2,0:T(8,128)(2,1)}), bf16[4,1024,256]{1,2,0:T(8,128)(2,1)}, u32[]{:S(2)}, u32[]{:S(2)}) async-start(bf16[4,1024,256]{1,2,0:T(8,128)(2,1)} %pad_maximum_fusion.14), calls=%async_computation.15 | async-start | bytes 4194304 | tf_op jit(solution)/shard_map/all_to_all | solution.py:399
  1390.8 67.8 %all-to-all-start.15 = ((bf16[4,1024,384]{1,2,0:T(8,128)(2,1)}), bf16[4,1024,384]{1,2,0:T(8,128)(2,1)}, u32[]{:S(2)}, u32[]{:S(2)}) async-start(bf16[4,1024,384]{1,2,0:T(8,128)(2,1)} %collective-permute-done.8), calls=%async_computation.17 | async-start | bytes 6291456 | tf_op jit(solution)/shard_map/all_to_all | solution.py:399
  1395.5 257.6 %reduce-scatter.15.cloned.1.call-start = ((), (), s32[]{:S(2)}) async-start(), calls=%async_computation.27 | async-start | bytes 10653696 | tf_op jit(solution)/shard_map/reduce_scatter | solution.py:455
  1489.0 216.3 %all-reduce.9.cloned.1.call-start = ((), (), s32[]{:S(2)}) async-start(), calls=%async_computation.38 | async-start | bytes 212992
  1615.1 193.4 %all-reduce.7.cloned.1.call-start = ((), (), s32[]{:S(2)}) async-start(), calls=%async_computation.29 | async-start | bytes 7520256 | tf_op jit(solution)/shard_map/psum | solution.py:458
  (182 other events, 4232.7 us)
Sparse Core Ops, SparseCore 0:
  18.5 75.6 all-gather.14
  96.4 71.2 all-gather.16
  169.3 31.4 all-gather.18
  202.4 90.0 all-gather.20
  294.5 94.0 all-gather.22
  390.1 31.3 all-gather.24
  423.2 90.0 all-gather.26
  515.5 94.0 all-gather.28
  738.5 105.9 reduce-scatter.18
  846.6 98.4 reduce-scatter.10
  1062.8 113.2 reduce-scatter.12
  1178.2 103.4 reduce-scatter.20
  1285.4 167.4 all-reduce.4
  1455.0 97.4 reduce-scatter.16
  1554.7 98.3 reduce-scatter.14
  1655.3 50.0 all-reduce.8
  1709.2 99.1 all-reduce.6

commit v3 on v2

--- a/solution.py
+++ b/solution.py
@@ -3,6 +3,7 @@
 from jax import lax
 from jax.experimental import pallas as pl
 from jax.experimental.pallas import tpu as pltpu
+from jax.experimental.layout import Layout, with_layout_constraint
 from jax.sharding import Mesh, PartitionSpec as P
 f32=jnp.float32; bf16=jnp.bfloat16
 NEG=-1e30
@@ -310,6 +311,10 @@
     return r * (y - a - xhat * b), jnp.sum(dn * xhat, axis=0), jnp.sum(dn, axis=0)
 
 
+def col_sum(x):
+    return jnp.dot(jnp.ones((16, x.shape[0]), bf16), x, preferred_element_type=f32)[0]
+
+
 def gelu_parts(u):
     z = jnp.abs(u) * 0.7071067811865476
     t = 1.0 / (1.0 + 0.3275911 * z)
@@ -348,7 +353,6 @@
     metas = [meta, swap(meta)][:S]
     phase_inv = [t[None, :NB] for t in metas]
     phase_nb = [t[NB:] for t in metas]
-    core = lax.axis_index("core")
     own = jnp.concatenate([inverse, lax.dynamic_slice_in_dim(order, 2 * me, 2, 0), count])
     own_pos = (lax.dynamic_slice_in_dim(order, 2 * me, 2, 0)[:, None] * B + jnp.arange(B, dtype=jnp.int32)).reshape(rows, 1)
     live = (own_pos < lengths[0]).astype(f32)
@@ -363,19 +367,20 @@
         return vec[:, layer, 8 * shard:].reshape(-1)
 
     def pack(w):
-        n = w.shape[0]
-        w = w.reshape(n, 3, HEADS, 64)
-        main = w[:, :, :16].reshape(n, 3, G, 128)
-        main = jnp.transpose(main, (0, 2, 1, 3)).reshape(n, G * 384)
-        tail = jnp.stack([w[:, 1, 16], w[:, 2, 16], w[:, 0, 16]], axis=1).reshape(n, 192)
-        return jnp.concatenate([main, tail], axis=1)
+        parts = []
+        for g in range(G):
+            parts += [w[:, kind * width + g * 128:kind * width + g * 128 + 128] for kind in range(3)]
+        last = width - 64
+        parts += [w[:, kind * width + last:kind * width + width] for kind in (1, 2, 0)]
+        return jnp.concatenate(parts, axis=1)
 
     def unpack(w):
-        n = w.shape[0]
-        main = jnp.transpose(w[:, :G * 384].reshape(n, G, 3, 128), (0, 2, 1, 3)).reshape(n, 3, 1024)
-        tail = w[:, G * 384:].reshape(n, 3, 64)
-        tail = jnp.stack([tail[:, 2], tail[:, 0], tail[:, 1]], axis=1)
-        return jnp.concatenate([main, tail], axis=2).reshape(n, 3 * width)
+        tail = G * 384
+        parts = []
+        for kind, last in enumerate((128, 0, 64)):
+            parts += [w[:, g * 384 + kind * 128:g * 384 + kind * 128 + 128] for g in range(G)]
+            parts.append(w[:, tail + last:tail + last + 64])
+        return jnp.concatenate(parts, axis=1)
 
     def fetch(w):
         return lax.all_gather(w.astype(bf16), FS, axis=0, tiled=True)
@@ -389,14 +394,11 @@
             fetch(down_weight[layer]),
         ))
 
-    def ordered(x, axis):
-        if S == 1:
-            return x
-        a, b = jnp.split(x, 2, axis=axis)
-        return jnp.where(core == 0, jnp.concatenate([a, b], axis), jnp.concatenate([b, a], axis))
+    def plain(x):
+        return with_layout_constraint(x, Layout(major_to_minor=tuple(range(x.ndim))))
 
     def exchange(x):
-        return lax.all_to_all(x, "ctx", 0, 0)
+        return plain(lax.all_to_all(plain(x), "ctx", 0, 0))
 
     def after(x, *others):
         return lax.optimization_barrier((x,) + others)
@@ -412,9 +414,9 @@
         wide = []
         for s in range(S):
             half = C * 384
-            first = half * (core if s == 0 else 1 - core) if S == 2 else 0
-            w = lax.dynamic_slice_in_dim(qkv_w, first, half, 1).reshape(width, C, 384)
-            b = lax.dynamic_slice_in_dim(bias, first, half, 0).reshape(C, 1, 384)
+            cols = slice(half * s, half * (s + 1))
+            w = qkv_w[:, cols].reshape(width, C, 384)
+            b = bias[cols].reshape(C, 1, 384)
             wide.append((jnp.einsum("rd,dgc->grc", n1, w, preferred_element_type=f32) + b).astype(bf16))
         if S == 2:
             wide[1] = swap(wide[1])
@@ -438,7 +440,7 @@
                 t, o_back[0] = after(t, o_back[0])
             o_back.append(exchange(swap(t) if s else t))
         o16, lse16 = one_fwd(q16, heads[-1][0], own, B)
-        o_all = ordered(jnp.concatenate(o_back, axis=0), 0)
+        o_all = jnp.concatenate(o_back, axis=0)
         mixed = jnp.concatenate([jnp.transpose(o_all, (1, 0, 2)).reshape(rows, HW), o16], axis=1)
         m = stream + jnp.dot(mixed, out_w, preferred_element_type=f32) + vector(4, layer)
         xhat2, _ = norm_parts(m)
@@ -464,32 +466,30 @@
 
     def finish(layer):
         d_four, d_up, d_down = fours[layer]
-        parts = [jnp.transpose(t.reshape(shard, 4, width), (1, 0, 2)).reshape(4 * shard, width) for t in (d_four, d_up)]
-        matrices[layer] = reduce_ctx(jnp.concatenate(parts + [d_down], axis=0))
+        matrices[layer] = tuple(t.astype(f32) for t in lax.psum((d_four, d_up, d_down), "ctx"))
 
     for layer in reversed(range(L)):
         stream_in, n1, heads, q16, o, lse, o16, lse16, mixed, m, n2, a, slope = records[layer]
         qkv_w, out_w, up_w, down_w = weights[layer]
         gb = grad.astype(bf16)
-        d_down_b = jnp.sum(gb.astype(f32), axis=0)
+        d_down_b = col_sum(gb)
         d_down = jnp.einsum("rf,rd->fd", a, gb, preferred_element_type=f32).astype(bf16)
-        gb, d_down = after(gb, d_down)
+        gb, d_down = after(gb, plain(d_down))
         d_down = reduce_fsdp(d_down)
         du = (jnp.einsum("rd,fd->rf", gb, down_w, preferred_element_type=f32) * slope.astype(f32)).astype(bf16)
-        d_up_b = jnp.sum(du.astype(f32), axis=0)
+        d_up_b = col_sum(du)
         d_up = jnp.einsum("rd,rf->df", n2, du, preferred_element_type=f32).astype(bf16)
-        du, d_up = after(du, d_up)
+        du, d_up = after(du, plain(d_up))
         d_up = reduce_fsdp(d_up)
         dn2 = jnp.einsum("rf,df->rd", du, up_w, preferred_element_type=f32)
         back, d_gain2, d_bias2 = norm_back(dn2, m, vector(5, layer))
         gm = grad + back
         gmb = gm.astype(bf16)
-        d_out_b = jnp.sum(gmb.astype(f32), axis=0)
+        d_out_b = col_sum(gmb)
         d_out = jnp.einsum("rd,re->de", mixed, gmb, preferred_element_type=f32).astype(bf16)
         d_o = []
         for s in range(S):
-            first = C * 128 * (core if s == 0 else 1 - core) if S == 2 else 0
-            w = lax.dynamic_slice_in_dim(out_w, first, C * 128, 0).reshape(C, 128, width)
+            w = out_w[C * 128 * s:C * 128 * (s + 1)].reshape(C, 128, width)
             d_o.append(jnp.einsum("re,gce->grc", gmb, w, preferred_element_type=f32).astype(bf16))
         d_o16 = jnp.einsum("re,ce->rc", gmb, out_w[HW:], preferred_element_type=f32).astype(bf16)
         dq16, dkv16 = one_bwd(q16, heads[-1][0], o16, d_o16, lse16, own, B)
@@ -500,9 +500,6 @@
                 t = swap(t)
             if s == S - 1:
                 t = jnp.concatenate([t, dkv16.reshape(C, rows, 128)], axis=2)
-            if s == S - 1 and layer < L - 1:
-                t, fours[layer + 1] = after(t, fours[layer + 1])
-                finish(layer + 1)
             if s:
                 t, d_oh[0] = after(t, d_oh[0])
             d_oh.append(exchange(t).reshape(1, N, -1))
@@ -512,24 +509,28 @@
             t = t.reshape(C, rows, 384)
             if s:
                 t, d_wide[0], d_down = after(t, d_wide[0], d_down)
+            if s == S - 1 and layer < L - 1:
+                done = after(t, *fours[layer + 1])
+                t, fours[layer + 1] = done[0], done[1:]
+                finish(layer + 1)
             d_wide.append(exchange(swap(t) if s else t))
-        d_wide = ordered(jnp.concatenate(d_wide, axis=0), 0)
+        d_wide = jnp.concatenate(d_wide, axis=0)
         d_tail = jnp.concatenate([dkv16.astype(bf16), dq16], axis=1)
         d_row = jnp.concatenate([jnp.transpose(d_wide, (1, 0, 2)).reshape(rows, G * 384), d_tail], axis=1)
+        d_row, d_up = after(d_row, d_up)
         d_qkv = jnp.einsum("rd,rc->dc", n1, d_row, preferred_element_type=f32).astype(bf16)
         d_four = jnp.concatenate([d_qkv, d_out], axis=1)
         if layer:
-            d_row, d_four = after(d_row, d_four)
-            d_row, d_up = after(d_row, d_up)
-        else:
-            d_four, matrices[layer + 1] = after(d_four, matrices[layer + 1])
+            d_row, d_four = after(d_row, plain(d_four))
         d_four = reduce_fsdp(d_four)
-        sums = unpack(jnp.sum(d_row.astype(f32), axis=0)[None])[0]
+        sums = unpack(col_sum(d_row)[None])[0]
         dn1 = jnp.einsum("rc,dc->rd", d_row, qkv_w, preferred_element_type=f32)
         back, d_gain1, d_bias1 = norm_back(dn1, stream_in, vector(0, layer))
         grad = gm + back
         fours[layer] = (d_four, d_up, d_down)
         if layer == 0:
+            done = after(d_four, d_up, d_down, *matrices[1])
+            fours[0], matrices[1] = done[:3], done[3:]
             finish(0)
         small[layer] = jnp.concatenate([
             t.reshape(-1, n) for t, n in (
@@ -541,14 +542,10 @@
     vec_grads = lax.psum(vec_grads, "ctx")[0]
     vg = [vec_grads[:, i * shard:(i + 1) * shard] for i in range(8)] + [vec_grads[:, 8 * shard:]]
 
-    def take(layer, start, cols):
-        t = matrices[layer][start * shard:(start + cols) * shard]
-        return jnp.transpose(t.reshape(cols, shard, width), (1, 0, 2)).reshape(shard, cols * width)
-
-    g_qkv = jnp.stack([unpack(take(layer, 0, 3)) for layer in range(L)])
-    g_out = jnp.stack([take(layer, 3, 1) for layer in range(L)])
-    g_up = jnp.stack([take(layer, 4, 4) for layer in range(L)])
-    g_down = jnp.stack([matrices[layer][8 * shard:] for layer in range(L)])
+    g_qkv = jnp.stack([unpack(matrices[layer][0][:, :3 * width]) for layer in range(L)])
+    g_out = jnp.stack([matrices[layer][0][:, 3 * width:] for layer in range(L)])
+    g_up = jnp.stack([matrices[layer][1] for layer in range(L)])
+    g_down = jnp.stack([matrices[layer][2] for layer in range(L)])
     return (activations, grad[None], vg[0], vg[1], g_qkv, vg[2], vg[3], g_out, vg[4], vg[5], vg[6], g_up, vg[8], g_down, vg[7])
 
 

time: 1860 us -> 1710 us (0.919)
  waiting for transfers between devices: 452 us -> 814 us
  Pallas kernels: 386 us -> 85.5 us
  local copies, waits for them, and re-layouts: 295 us -> 128 us
  other arithmetic: 166 us -> 132 us
  matrix products: 399 us -> 430 us
  starting transfers between devices: 98.6 us -> 69.3 us
    all_to_all x15 -> x16, waiting for transfers between devices: 96.9 us -> 286 us  [exchange(): return plain(lax.all_to_all(plain(x), 'ctx', 0, 0))]
    reduce_scatter x4 -> x6, waiting for transfers between devices: 73.8 us -> 253 us  [reduce_fsdp(): return lax.psum_scatter(g.astype(bf16), FS, scatter_dimension=0, tiled=True)]
    pallas_call x4, Pallas kernels: 205 us -> 48 us  [flash_bwd(): pl.pallas_call(functools.partial(bwd_kernel, B=B, NB=NB), out_shape=jax.S...]
    pallas_call x4, Pallas kernels: 133 us -> 29.2 us  [flash_fwd(): pl.pallas_call(functools.partial(fwd_kernel, B=B, NB=NB), out_shape=(jax....]
    reshape x36 -> x0, local copies, waits for them, and re-layouts: 58.7 us -> none  [the longest x8 21.3 us: finish(): t.reshape(shard, 4, width)]
    dynamic_slice x8 -> x0, local copies, waits for them, and re-layouts: 40.3 us -> none  [the longest x5 35.4 us: local(): w = lax.dynamic_slice_in_dim(qkv_w, first, half, 1).reshape(width, C, 384)]
    unnamed x337 -> x306, local copies, waits for them, and re-layouts: 64.3 us -> 27.2 us
    reduce_sum x6 -> x0, other arithmetic: 35.2 us -> none  [the longest x2 13.8 us: local(): d_down_b = jnp.sum(gb.astype(f32), axis=0)]
  transfers between devices with their start and end apart: 41 -> 42, of which waited for: 16 -> 30; matrix products, arithmetic and copies ran while one was open for 41% -> 34% of each run, Pallas kernels for 21% -> 5%
where the time goes in v3:
time: 1710 us
  waiting for transfers between devices  814 us (48%)
  matrix products  430 us (25%)
  other arithmetic  132 us (8%)
  local copies, waits for them, and re-layouts  128 us (7%)
  Pallas kernels  85.5 us (5%)
  starting transfers between devices  69.3 us (4%)
  blocking collectives  32.4 us (2%)
  between operations  17.3 us (1%)
    all_to_all x16, waiting for transfers between devices, exchange(): return plain(lax.all_to_all(plain(x), 'ctx', 0, 0))  286 us
    reduce_scatter x6, waiting for transfers between devices, reduce_fsdp(): return lax.psum_scatter(g.astype(bf16), FS, scatter_dimension=0, tiled=True)  253 us
    all_gather x8, waiting for transfers between devices, fetch(): return lax.all_gather(w.astype(bf16), FS, axis=0, tiled=True)  120 us
    psum x2, waiting for transfers between devices, finish(): lax.psum((d_four, d_up, d_down), 'ctx')  108 us
    dot_general x2, matrix products, local(): u = jnp.dot(n2, up_w, preferred_element_type=f32) + vector(8, layer)  70.5 us
    all_to_all x16, starting transfers between devices, exchange(): return plain(lax.all_to_all(plain(x), 'ctx', 0, 0))  66.6 us
    dot_general x2, matrix products, local(): jnp.einsum('rd,fd->rf', gb, down_w, preferred_element_type=f32)  59.4 us
    pallas_call x4, Pallas kernels, flash_bwd(): pl.pallas_call(functools.partial(bwd_kernel, B=B, NB=NB), out_shape=jax.S...  48 us
  transfers between devices with their start and end apart: 42, of which 30 were waited for; matrix products, arithmetic and copies ran while one was open for 34% of the time, Pallas kernels for 5%

profile of v3, /device:TPU:0, one launch (start us, length us, event | category | flops | bytes accessed | tf_op | source)
XLA Modules:
  0.0 1708.8 jit_solution(10294759974743746367)
XLA Ops:
  46.9 42.0 %all-gather.15.cloned.1.call-done = bf16[1088,3264]{1,0:T(8,128)(2,1)} async-done(((bf16[136,3264]{1,0:T(8,128)(2,1)}), bf16[1088,3264]{1,0:T(8,128)(2,1)}) %all-gather.15.cloned.1.call-update) | async-done | bytes 7102480 | tf_op jit(solution)/shard_map/all_gather | solution.py:386
  135.6 27.4 %all-to-all-done = bf16[4,1024,384]{2,1,0:T(8,128)(2,1)S(1)} async-done(((bf16[4,1024,384]{2,1,0:T(8,128)(2,1)}), bf16[4,1024,384]{2,1,0:T(8,128)(2,1)S(1)}, u32[]{:S(2)}, u32[]{:S(2)}) %all-to-all-start) | async-done | bytes 3145760 | tf_op jit(solution)/shard_map/all_to_all | solution.py:401
  177.2 37.9 %all-to-all-done.1 = bf16[4,1024,512]{2,1,0:T(8,128)(2,1)} async-done(((bf16[4,1024,512]{2,1,0:T(8,128)(2,1)}), bf16[4,1024,512]{2,1,0:T(8,128)(2,1)}, u32[]{:S(2)}, u32[]{:S(2)}) %all-to-all-start.1) | async-done | bytes 4194336 | tf_op jit(solution)/shard_map/all_to_all | solution.py:401
  286.8 35.1 %multiply_convert_fusion.3 = (bf16[1024,4352]{1,0:T(8,128)(2,1)}, f32[1024,4352]{1,0:T(8,128)}) fusion(f32[4352]{0:T(1024)S(1)} %add.346, bf16[1,1088,4352]{2,1,0:T(8,128)(2,1)} %all-gather.21.cloned.1.call-done, f32[1024,1088]{0,1:T(8,128)} %copy-done.52, f32[1088]{0:T(1024)S(1)} %add.343, f32[1088]{0:T(1024)S(1)} %mul.346, f32[1024]{0:T(1024)S(1)} %add_rsqrt_fusion.2, ...), kind=kOutput, calls=%fused_computation.15 | convolution fusion | flops 9809756160 | bytes 40699392 | tf_op jit(solution)/shard_map/dot_general | solution.py:448
  321.9 60.4 %all-gather.23.cloned.1.call-done = bf16[1,4352,1088]{2,1,0:T(8,128)(2,1)} async-done(((bf16[1,544,1088]{2,1,0:T(8,128)(2,1)}), bf16[1,4352,1088]{2,1,0:T(8,128)(2,1)}) %all-gather.23.cloned.1.call-update) | async-done | bytes 9469968 | tf_op jit(solution)/shard_map/all_gather | solution.py:386
  437.2 27.9 %all-to-all-done.4 = bf16[4,1024,384]{2,1,0:T(8,128)(2,1)S(1)} async-done(((bf16[4,1024,384]{2,1,0:T(8,128)(2,1)}), bf16[4,1024,384]{2,1,0:T(8,128)(2,1)S(1)}, u32[]{:S(2)}, u32[]{:S(2)}) %all-to-all-start.4) | async-done | bytes 3145760 | tf_op jit(solution)/shard_map/all_to_all | solution.py:401
  476.0 41.4 %all-to-all-done.5 = bf16[4,1024,512]{2,1,0:T(8,128)(2,1)} async-done(((bf16[4,1024,512]{2,1,0:T(8,128)(2,1)}), bf16[4,1024,512]{2,1,0:T(8,128)(2,1)}, u32[]{:S(2)}, u32[]{:S(2)}) %all-to-all-start.5) | async-done | bytes 4194336 | tf_op jit(solution)/shard_map/all_to_all | solution.py:401
  572.1 35.3 %multiply_convert_fusion.2 = (bf16[1024,4352]{1,0:T(8,128)(2,1)}, f32[1024,4352]{1,0:T(8,128)}) fusion(f32[4352]{0:T(1024)S(1)} %add.379, bf16[1,1088,4352]{2,1,0:T(8,128)(2,1)} %all-gather.27.cloned.1.call-done, f32[1024,1088]{0,1:T(8,128)} %copy-done.39, f32[1088]{0:T(1024)S(1)} %add.376, f32[1088]{0:T(1024)S(1)} %mul.370, f32[1024]{0:T(1024)S(1)} %add_rsqrt_fusion, ...), kind=kOutput, calls=%fused_computation.14 | convolution fusion | flops 9809756160 | bytes 40699392 | tf_op jit(solution)/shard_map/dot_general | solution.py:448
  625.1 31.3 %multiply_convert_fusion.1 = bf16[1024,4352]{1,0:T(8,128)(2,1)} fusion(bf16[1024,1088]{0,1:T(8,128)(2,1)} %fusion.55, bf16[1,4352,1088]{2,1,0:T(8,128)(2,1)} %all-gather.29.cloned.1.call-done, f32[1024,4352]{1,0:T(8,128)} %get-tuple-element.408, f32[4352]{0:T(1024)S(1)} %add.379), kind=kOutput, calls=%fused_computation.12 | convolution fusion | flops 9826467840 | bytes 38454272 | tf_op jit(solution)/shard_map/rd,fd->rf/dot_general | solution.py:479
  656.4 18.0 %convolution_convert_fusion.2 = bf16[1088,4352]{1,0:T(8,128)(2,1)} fusion(bf16[1024,4352]{1,0:T(8,128)(2,1)} %multiply_convert_fusion.1, f32[1024,1088]{0,1:T(8,128)} %copy-done.39, f32[1088]{0:T(1024)S(1)} %add.376, f32[1088]{0:T(1024)S(1)} %mul.370, f32[1024]{0:T(1024)S(1)} %add_rsqrt_fusion, f32[1024]{0:T(1024)S(1)} %broadcast_multiply_fusion.8), kind=kOutput, calls=%fused_computation.6 | convolution fusion | flops 9707536384 | bytes 22856192 | tf_op jit(solution)/shard_map/rd,rf->df/dot_general | solution.py:481
  676.4 19.3 %multiply_reduce_fusion = (f32[1088]{0:T(1024)}, f32[1024]{0:T(1024)S(1)}, f32[1024]{0:T(1024)S(1)}, f32[1088]{0:T(1024)}, f32[1024,1088]{0,1:T(8,128)S(1)}) fusion(f32[1024,1088]{0,1:T(8,128)} %copy-done.39, f32[1024]{0:T(1024)S(1)} %add_rsqrt_fusion, f32[1024]{0:T(1024)S(1)} %broadcast_multiply_fusion.8, f32[1088]{0:T(1024)S(1)} %mul.370, ...), kind=kOutput, calls=%fused_computation.81 | convolution fusion | flops 9707253760 | bytes 27325184 | tf_op jit(solution)/shard_map/rf,df->rd/dot_general | solution.py:484
  772.7 19.1 %all-to-all-done.10 = bf16[4,1024,384]{2,1,0:T(8,128)(2,1)} async-done(((bf16[4,1024,384]{2,1,0:T(8,128)(2,1)}), bf16[4,1024,384]{2,1,0:T(8,128)(2,1)}, u32[]{:S(2)}, u32[]{:S(2)}) %all-to-all-start.10) | async-done | bytes 3145760 | tf_op jit(solution)/shard_map/all_to_all | solution.py:401
  810.3 29.3 %all-to-all-done.11 = bf16[4,1024,384]{2,1,0:T(8,128)(2,1)} async-done(((bf16[4,1024,384]{2,1,0:T(8,128)(2,1)}), bf16[4,1024,384]{2,1,0:T(8,128)(2,1)}, u32[]{:S(2)}, u32[]{:S(2)}) %all-to-all-start.11) | async-done | bytes 3145760 | tf_op jit(solution)/shard_map/all_to_all | solution.py:401
  929.0 28.1 %multiply_convert_fusion = bf16[1024,4352]{1,0:T(8,128)(2,1)} fusion(bf16[1024,1088]{0,1:T(8,128)(2,1)S(1)} %copy-done.57, bf16[1,4352,1088]{2,1,0:T(8,128)(2,1)} %all-gather.23.cloned.1.call-done, f32[1024,4352]{1,0:T(8,128)} %get-tuple-element.402, f32[4352]{0:T(1024)S(1)} %copy-done.102), kind=kOutput, calls=%fused_computation.10 | convolution fusion | flops 9826467840 | bytes 38454272 | tf_op jit(solution)/shard_map/rd,fd->rf/dot_general | solution.py:479
  975.9 19.2 %multiply_reduce_fusion.2 = (f32[1088]{0:T(1024)}, f32[1024]{0:T(1024)S(1)}, f32[1024]{0:T(1024)S(1)}, f32[1088]{0:T(1024)S(1)}, f32[1024,1088]{0,1:T(8,128)S(1)}) fusion(f32[1024,1088]{0,1:T(8,128)} %copy-done.52, f32[1024]{0:T(1024)S(1)} %copy-done.106, f32[1024]{0:T(1024)S(1)} %copy-done.92, f32[1088]{0:T(1024)S(1)} %copy-done.96, ...), kind=kOutput, calls=%fused_computation.83 | convolution fusion | flops 9707253760 | bytes 27325184 | tf_op jit(solution)/shard_map/rf,df->rd/dot_general | solution.py:484
  1073.4 20.1 %all-to-all-done.14 = bf16[4,1024,384]{2,1,0:T(8,128)(2,1)} async-done(((bf16[4,1024,384]{2,1,0:T(8,128)(2,1)}), bf16[4,1024,384]{2,1,0:T(8,128)(2,1)}, u32[]{:S(2)}, u32[]{:S(2)}) %all-to-all-start.14) | async-done | bytes 3145760 | tf_op jit(solution)/shard_map/all_to_all | solution.py:401
  1093.4 31.8 %reduce-scatter.11.cloned.1.call-done = bf16[544,1088]{1,0:T(8,128)(2,1)} async-done(((bf16[4352,1088]{1,0:T(8,128)(2,1)}), bf16[544,1088]{1,0:T(8,128)(2,1)}) %reduce-scatter.11.cloned.1.call-update) | async-done | bytes 1183760 | tf_op jit(solution)/shard_map/reduce_scatter | solution.py:457
  1125.2 100.6 %reduce-scatter.13.cloned.1.call-done = bf16[136,4352]{1,0:T(8,128)(2,1)} async-done(((bf16[1088,4352]{1,0:T(8,128)(2,1)}), bf16[136,4352]{1,0:T(8,128)(2,1)}) %reduce-scatter.13.cloned.1.call-update) | async-done | bytes 1183760 | tf_op jit(solution)/shard_map/reduce_scatter | solution.py:457
  1244.2 29.0 %all-to-all-done.15 = bf16[4,1024,384]{2,1,0:T(8,128)(2,1)} async-done(((bf16[4,1024,384]{2,1,0:T(8,128)(2,1)}), bf16[4,1024,384]{2,1,0:T(8,128)(2,1)}, u32[]{:S(2)}, u32[]{:S(2)}) %all-to-all-start.15) | async-done | bytes 3145760 | tf_op jit(solution)/shard_map/all_to_all | solution.py:401
  1301.2 25.4 %reduce-scatter.15.cloned.1.call-done = bf16[136,4352]{1,0:T(8,128)(2,1)} async-done(((bf16[1088,4352]{1,0:T(8,128)(2,1)}), bf16[136,4352]{1,0:T(8,128)(2,1)}) %reduce-scatter.15.cloned.1.call-update) | async-done | bytes 1183760 | tf_op jit(solution)/shard_map/reduce_scatter | solution.py:457
  1389.6 34.3 %all-reduce.11.cloned.1.call-done = (bf16[136,4352]{1,0:T(8,128)(2,1)}, bf16[136,4352]{1,0:T(8,128)(2,1)}, bf16[544,1088]{1,0:T(8,128)(2,1)}) async-done(((bf16[136,4352]{1,0:T(8,128)(2,1)}, bf16[136,4352]{1,0:T(8,128)(2,1)}, bf16[544,1088]{1,0:T(8,128)(2,1)}), (bf16[136,4352]{1,0:T(8,128)(2,1)}, bf16[136,4352]{1,0:T(8,128)(2,1)}, bf16[544,1088]{1,0:T(8,128)(2,1)})) %all-reduce.11.cloned.1.call-update) | async-done | bytes 3551248 | tf_op jit(solution)/shard_map/psum | solution.py:469
  1431.5 94.9 %reduce-scatter.17.cloned.1.call-done = bf16[136,4352]{1,0:T(8,128)(2,1)} async-done(((bf16[1088,4352]{1,0:T(8,128)(2,1)}), bf16[136,4352]{1,0:T(8,128)(2,1)}) %reduce-scatter.17.cloned.1.call-update) | async-done | bytes 1183760 | tf_op jit(solution)/shard_map/reduce_scatter | solution.py:457
  1550.9 28.2 %all-reduce.7.cloned.1.call-done = f32[8,2,1632]{2,1,0:T(2,128)} async-done(((f32[8,2,1632]{2,1,0:T(2,128)}), f32[8,2,1632]{2,1,0:T(2,128)}) %all-reduce.7.cloned.1.call-update) | async-done | bytes 104464
  1606.5 73.6 %all-reduce.9.cloned.1.call-done = (bf16[136,4352]{1,0:T(8,128)(2,1)}, bf16[1,136,4352]{2,1,0:T(8,128)(2,1)}, bf16[1,544,1088]{2,1,0:T(8,128)(2,1)}) async-done(((bf16[136,4352]{1,0:T(8,128)(2,1)}, bf16[1,136,4352]{2,1,0:T(8,128)(2,1)}, bf16[1,544,1088]{2,1,0:T(8,128)(2,1)}), (bf16[136,4352]{1,0:T(8,128)(2,1)}, bf16[1,136,4352]{2,1,0:T(8,128)(2,1)}, ...) | async-done | bytes 3551248 | tf_op jit(solution)/shard_map/psum | solution.py:469
  (626 shorter events, 781.7 us)
Async XLA Ops:
  7.2 81.8 %all-gather.15.cloned.1.call-start = ((), (), s32[]{:S(2)}) async-start(), calls=%async_computation.22 | async-start | bytes 8146944 | tf_op jit(solution)/shard_map/all_gather | solution.py:386
  13.2 225.6 %all-gather.17.cloned.1.call-start = ((), (), s32[]{:S(2)}) async-start(), calls=%async_computation.23 | async-start | bytes 8146944 | tf_op jit(solution)/shard_map/all_gather | solution.py:386
  16.7 243.6 %all-gather.19.cloned.1.call-start = ((), (), s32[]{:S(2)}) async-start(), calls=%async_computation.30 | async-start | bytes 2820096 | tf_op jit(solution)/shard_map/all_gather | solution.py:386
  17.8 269.0 %all-gather.21.cloned.1.call-start = ((), (), s32[]{:S(2)}) async-start(), calls=%async_computation.31 | async-start | bytes 10653696 | tf_op jit(solution)/shard_map/all_gather | solution.py:386
  22.0 360.4 %all-gather.23.cloned.1.call-start = ((), (), s32[]{:S(2)}) async-start(), calls=%async_computation.32 | async-start | bytes 11280384 | tf_op jit(solution)/shard_map/all_gather | solution.py:386
  26.9 535.2 %all-gather.25.cloned.1.call-start = ((), (), s32[]{:S(2)}) async-start(), calls=%async_computation.33 | async-start | bytes 2820096 | tf_op jit(solution)/shard_map/all_gather | solution.py:386
  122.4 40.7 %all-to-all-start = ((bf16[4,1024,384]{2,1,0:T(8,128)(2,1)}), bf16[4,1024,384]{2,1,0:T(8,128)(2,1)S(1)}, u32[]{:S(2)}, u32[]{:S(2)}) async-start(bf16[4,1024,384]{2,1,0:T(8,128)(2,1)} %fusion.63), calls=%async_computation | async-start | bytes 6291456 | tf_op jit(solution)/shard_map/all_to_all | solution.py:401
  163.0 52.1 %all-to-all-start.1 = ((bf16[4,1024,512]{2,1,0:T(8,128)(2,1)}), bf16[4,1024,512]{2,1,0:T(8,128)(2,1)}, u32[]{:S(2)}, u32[]{:S(2)}) async-start(bf16[4,1024,512]{2,1,0:T(8,128)(2,1)} %pad_maximum_fusion.6), calls=%async_computation.1 | async-start | bytes 8388608 | tf_op jit(solution)/shard_map/all_to_all | solution.py:401
  167.9 404.2 %all-gather.27.cloned.1.call-start = ((), (), s32[]{:S(2)}) async-start(), calls=%async_computation.34 | async-start | bytes 10653696 | tf_op jit(solution)/shard_map/all_gather | solution.py:386
  424.5 40.7 %all-to-all-start.4 = ((bf16[4,1024,384]{2,1,0:T(8,128)(2,1)}), bf16[4,1024,384]{2,1,0:T(8,128)(2,1)S(1)}, u32[]{:S(2)}, u32[]{:S(2)}) async-start(bf16[4,1024,384]{2,1,0:T(8,128)(2,1)} %fusion.65), calls=%async_computation.4 | async-start | bytes 6291456 | tf_op jit(solution)/shard_map/all_to_all | solution.py:401
  428.4 196.7 %all-gather.29.cloned.1.call-start = ((), (), s32[]{:S(2)}) async-start(), calls=%async_computation.35 | async-start | bytes 11280384 | tf_op jit(solution)/shard_map/all_gather | solution.py:386
  465.2 52.3 %all-to-all-start.5 = ((bf16[4,1024,512]{2,1,0:T(8,128)(2,1)}), bf16[4,1024,512]{2,1,0:T(8,128)(2,1)}, u32[]{:S(2)}, u32[]{:S(2)}) async-start(bf16[4,1024,512]{2,1,0:T(8,128)(2,1)} %pad_maximum_fusion.7), calls=%async_computation.5 | async-start | bytes 8388608 | tf_op jit(solution)/shard_map/all_to_all | solution.py:401
  541.2 250.6 %reduce-scatter.7.cloned.1.call-start = ((), (), s32[]{:S(2)}) async-start(), calls=%async_computation.24 | async-start | bytes 11280384 | tf_op jit(solution)/shard_map/reduce_scatter | solution.py:457
  625.0 242.4 %reduce-scatter.9.cloned.1.call-start = ((), (), s32[]{:S(2)}) async-start(), calls=%async_computation.25 | async-start | bytes 10653696 | tf_op jit(solution)/shard_map/reduce_scatter | solution.py:457
  751.3 40.4 %all-to-all-start.10 = ((bf16[4,1024,384]{2,1,0:T(8,128)(2,1)}), bf16[4,1024,384]{2,1,0:T(8,128)(2,1)}, u32[]{:S(2)}, u32[]{:S(2)}) async-start(bf16[4,1024,384]{2,1,0:T(8,128)(2,1)} %bitcast.301), calls=%async_computation.10 | async-start | bytes 6291456 | tf_op jit(solution)/shard_map/all_to_all | solution.py:401
  798.2 41.4 %all-to-all-start.11 = ((bf16[4,1024,384]{2,1,0:T(8,128)(2,1)}), bf16[4,1024,384]{2,1,0:T(8,128)(2,1)}, u32[]{:S(2)}, u32[]{:S(2)}) async-start(bf16[4,1024,384]{2,1,0:T(8,128)(2,1)} %collective-permute-done.6), calls=%async_computation.12 | async-start | bytes 6291456 | tf_op jit(solution)/shard_map/all_to_all | solution.py:401
  802.8 322.4 %reduce-scatter.11.cloned.1.call-start = ((), (), s32[]{:S(2)}) async-start(), calls=%async_computation.26 | async-start | bytes 11280384 | tf_op jit(solution)/shard_map/reduce_scatter | solution.py:457
  927.3 298.5 %reduce-scatter.13.cloned.1.call-start = ((), (), s32[]{:S(2)}) async-start(), calls=%async_computation.27 | async-start | bytes 10653696 | tf_op jit(solution)/shard_map/reduce_scatter | solution.py:457
  927.9 398.7 %reduce-scatter.15.cloned.1.call-start = ((), (), s32[]{:S(2)}) async-start(), calls=%async_computation.28 | async-start | bytes 10653696 | tf_op jit(solution)/shard_map/reduce_scatter | solution.py:457
  1231.8 41.4 %all-to-all-start.15 = ((bf16[4,1024,384]{2,1,0:T(8,128)(2,1)}), bf16[4,1024,384]{2,1,0:T(8,128)(2,1)}, u32[]{:S(2)}, u32[]{:S(2)}) async-start(bf16[4,1024,384]{2,1,0:T(8,128)(2,1)} %collective-permute-done.8), calls=%async_computation.19 | async-start | bytes 6291456 | tf_op jit(solution)/shard_map/all_to_all | solution.py:401
  1236.5 187.5 %all-reduce.11.cloned.1.call-start = ((), (), s32[]{:S(2)}) async-start(), calls=%async_computation.38 | async-start | bytes 7241728 | tf_op jit(solution)/shard_map/psum | solution.py:469
  1243.8 282.6 %reduce-scatter.17.cloned.1.call-start = ((), (), s32[]{:S(2)}) async-start(), calls=%async_computation.29 | async-start | bytes 10653696 | tf_op jit(solution)/shard_map/reduce_scatter | solution.py:457
  1344.4 234.8 %all-reduce.7.cloned.1.call-start = ((), (), s32[]{:S(2)}) async-start(), calls=%async_computation.36 | async-start | bytes 212992
  1388.7 291.5 %all-reduce.9.cloned.1.call-start = ((), (), s32[]{:S(2)}) async-start(), calls=%async_computation.37 | async-start | bytes 7241728 | tf_op jit(solution)/shard_map/psum | solution.py:469
  (151 other events, 3764.1 us)
Sparse Core Ops, SparseCore 0:
  13.3 75.6 all-gather.14
  90.6 71.2 all-gather.16
  163.5 31.4 all-gather.18
  196.5 90.1 all-gather.20
  288.2 94.0 all-gather.22
  383.8 33.0 all-gather.24
  418.6 89.4 all-gather.26
  510.3 94.0 all-gather.28
  625.1 133.7 reduce-scatter.6
  761.1 98.4 reduce-scatter.8
  927.4 197.7 reduce-scatter.10
  1127.4 98.4 reduce-scatter.12
  1228.1 98.4 reduce-scatter.14
  1329.9 93.9 all-reduce.10
  1426.1 100.2 reduce-scatter.16
  1529.2 49.9 all-reduce.6
  1582.9 97.2 all-reduce.8
